TPU v7x, 128 devices: a whole 4x4x4 slice. The times are simulated.
128 devices in a mesh: row: 32 (over y, z, core), col: 4 (over x).
Axes of the slice: x: 4, y: 4, z: 4, core: 2. Of those that a mesh axis runs over, the one named last changes fastest.
Arguments:
- coupling: float32 [4096, 61440], P('row', 'col'), may hold values from 0.1 to 10
- src_left: bfloat16 [4096, 128], P('row'), may hold values from -8 to 8
- emitter_distance_rightside: bfloat16 [4096, 128], P('row'), may hold values from -0.09375 to 0.09375
- destination_distance_leftside: bfloat16 [128, 61440], P('row', 'col'), may hold values from -2 to 2
- tgt_right: bfloat16 [128, 61440], P('row', 'col'), may hold values from -0.0234375 to 0.0234375
- log_src: float32 [4096], P('row'), may hold values from -1 to 1
- logarithm_destination_masses: float32 [61440], P('col'), may hold values from -1 to 1
- tgt_potential: float32 [61440], P('col'), may hold values from -12 to 12
Outputs:
- refreshed_plan_matrix: float32 [4096, 61440], P('row', 'col')
- row_potential: float32 [4096], P('row')
- col_potential: float32 [61440], P('col')
All inputs are finite; a program needn't handle non-finite values.
Results may differ from a plain program's by a relative error of at most 0.035.
The roundings to bfloat16 on the way count: a program that leaves them out, or rounds other values in their place, can miss the bound.
Values may be sent and summed in bfloat16 or wider, within the bound.
A program may use at most 64 MiB of HBM per device.

v0:
```python
import jax
import jax.numpy as jnp
from jax import lax
from jax.sharding import PartitionSpec as P

regularization_strength = 4.0


def merged(array, axis, combine):
    everything = jax.tree.map(lambda part: lax.all_gather(part, axis), array)
    leading = jax.tree.map(lambda part: part[0], everything)

    def step(k, so_far):
        return combine(so_far, jax.tree.map(lambda part: part[k], everything))

    return lax.fori_loop(1, lax.axis_size(axis), step, leading)


def for_sending(array):

    def short(part):
        return part.astype(jnp.bfloat16) if part.dtype == jnp.float32 else part

    return jax.tree.map(short, array)


def merge_pairs(first, second):
    peak_one, total_one = first
    peak_two, total_two = second
    peak = jnp.maximum(peak_one, peak_two)
    total = total_one * jnp.exp(peak_one - peak) + total_two * jnp.exp(peak_two - peak)
    return (peak, total)


def per_device(
    coupling,
    src_left,
    emitter_distance_rightside,
    destination_distance_leftside,
    tgt_right,
    log_src,
    logarithm_destination_masses,
    tgt_potential,
):
    highest = lax.Precision.HIGHEST
    carried = lax.dot_general(
        coupling,
        lax.all_gather(tgt_right, "row", axis=0, tiled=True).astype(jnp.float32),
        (((1,), (1,)), ((), ())),
        precision=highest,
    )
    source_right = emitter_distance_rightside.astype(jnp.float32)
    contract = (((0,), (0,)), ((), ()))
    partial_core_product = lax.dot_general(source_right, carried, contract, precision=highest)
    rank_core = lax.psum(partial_core_product, ("row", "col"))
    price_matrix_slab = jnp.dot(
        src_left, rank_core.astype(jnp.bfloat16), preferred_element_type=jnp.float32
    ).astype(jnp.bfloat16)
    divided_price_matrix = jnp.dot(
        price_matrix_slab,
        lax.all_gather(destination_distance_leftside, "row", axis=0, tiled=True),
        preferred_element_type=jnp.float32,
    ) * (-2.0 / regularization_strength)
    row_scores = tgt_potential[None, :] - divided_price_matrix
    row_peak = jnp.max(row_scores, axis=1)
    row_total = jnp.sum(jnp.exp(row_scores - row_peak[:, None]), axis=1)
    row_peak, row_total = merged((row_peak, row_total), "col", merge_pairs)
    row_potential = log_src - (row_peak + jnp.log(row_total))
    col_scores = row_potential[:, None] - divided_price_matrix
    col_peak = lax.pmax(for_sending(jnp.max(col_scores, axis=0)), "row")
    column_mass_sum = lax.psum(
        jnp.sum(jnp.exp(col_scores - col_peak[None, :]), axis=0).astype(jnp.bfloat16), "row"
    ).astype(jnp.float32)
    col_potential = logarithm_destination_masses - (col_peak + jnp.log(column_mass_sum))
    source_count = coupling.shape[0] * lax.axis_size("row")
    refreshed_plan_matrix = source_count * jnp.exp(
        row_potential[:, None] + col_potential[None, :] - divided_price_matrix
    )
    return (refreshed_plan_matrix, row_potential, col_potential)


def solution(mesh):
    return jax.shard_map(
        per_device,
        mesh=mesh,
        in_specs=(
            P("row", "col"),
            P("row", None),
            P("row", None),
            P("row", "col"),
            P("row", "col"),
            P("row"),
            P("col"),
            P("col"),
        ),
        out_specs=(P("row", "col"), P("row"), P("col")),
        check_vma=False,
    )
```

profile of v0, /device:TPU:1, one launch (start us, length us, event | category | flops | bytes accessed | tf_op | source)
XLA Modules:
  0.0 439.5 jit_solution(1108674910085604998)
XLA Ops:
  7.2 0.0 copy-start
  7.2 0.0 all-gather.9.cloned.1.call-start
  7.2 0.7 all-gather.9.cloned.1.call-update
  7.9 0.0 all-gather.11.cloned.1.call-start
  8.0 0.7 all-gather.11.cloned.1.call-update
  8.7 51.2 %all-gather.9.cloned.1.call-done = bf16[32,4,15360]{2,1,0:T(4,128)(2,1)} async-done(((bf16[1,4,15360]{2,1,0:T(4,128)(2,1)}), bf16[32,4,15360]{2,1,0:T(4,128)(2,1)}) %all-gather.9.cloned.1.call-update) | async-done | bytes 3932176 | tf_op jit(solution)/shard_map/all_gather | solution.py:48
  59.8 6.3 %reshape.19 = bf16[128,15360]{1,0:T(8,128)(2,1)} reshape(bf16[32,4,15360]{2,1,0:T(4,128)(2,1)} %all-gather.9.cloned.1.call-done) | data formatting | bytes 7864320
  66.1 0.0 copy-start.4
  66.1 0.0 copy-start.1
  66.1 8.0 %fusion.4 = f32[128,128]{1,0:T(8,128)S(1)} fusion(f32[128,15360]{1,0:T(8,128)} %param.10, bf16[128,15360]{1,0:T(8,128)(2,1)} %reshape.19), kind=kOutput, calls=%fused_computation.19 | convolution fusion | flops 3019898880 | bytes 11862016 | tf_op jit(solution)/shard_map/dot_general | solution.py:46
  74.1 0.0 copy-done.4
  74.1 0.3 convolution_bitcast_fusion
  74.4 64.7 %psum.14 = bf16[128,128]{0,1:T(8,128)(2,1)S(1)} all-reduce(f32[128,128]{0,1:T(8,128)S(1)} %convolution_bitcast_fusion), channel_id=1, replica_groups=mesh['row'=32,'col'=4] {'row','col'}, use_global_device_ids=true, to_apply=%region_0.0 | all-reduce | flops 16384 | bytes 98304 | tf_op jit(solution)/shard_map/psum | solution.py:55
  139.1 0.0 all-gather.11.cloned.1.call-done
  139.1 6.3 %reshape.21 = bf16[128,15360]{1,0:T(8,128)(2,1)} reshape(bf16[32,4,15360]{2,1,0:T(4,128)(2,1)} %all-gather.11.cloned.1.call-done) | data formatting | bytes 7864320
  145.4 0.0 copy-done
  145.4 0.0 copy-done.1
  145.4 0.0 copy-start.6
  145.4 6.8 %subtract_reduce_fusion.1 = (f32[128]{0:T(128)S(1)}, f32[128,15360]{1,0:T(8,128)}) fusion(f32[15360]{0:T(1024)S(1)} %copy-done.1, bf16[128,15360]{1,0:T(8,128)(2,1)} %reshape.21, bf16[128,128]{1,0:T(8,128)(2,1)S(1)} %copy-done, bf16[128,128]{0,1:T(8,128)(2,1)S(1)} %psum.14), kind=kOutput, calls=%fused_computation.11 | convolution fusion | flops 513425280 | bytes 11923968 | tf_op jit(solution)/shard_map/dot_general | solution.py:59
  152.2 4.7 %exponential_reduce_fusion.1 = f32[128]{0:T(128)S(1)} fusion(f32[128,15360]{1,0:T(8,128)} %get-tuple-element.151, f32[128]{0:T(128)S(1)} %get-tuple-element.150, f32[15360]{0:T(1024)S(1)} %copy-done.1), kind=kLoop, calls=%fused_computation.9 | loop fusion | flops 5898112 | bytes 7926784 | tf_op jit(solution)/shard_map/reduce_sum | solution.py:66
  156.9 7.0 %all-gather.5 = f32[4,1,128]{2,1,0:T(1,128)S(1)} all-gather(f32[1,1,128]{2,1,0:T(1,128)S(1)} %bitcast.38), channel_id=3, replica_groups=mesh['row'=32,'col'=4] {'col'}, dimensions={0}, use_global_device_ids=true | all-gather | bytes 2560 | tf_op jit(solution)/shard_map/all_gather | solution.py:10
  163.9 5.2 %all-gather.4 = f32[4,1,128]{2,1,0:T(1,128)S(1)} all-gather(f32[1,1,128]{2,1,0:T(1,128)S(1)} %bitcast.37), channel_id=2, replica_groups=mesh['row'=32,'col'=4] {'col'}, dimensions={0}, use_global_device_ids=true | all-gather | bytes 2560 | tf_op jit(solution)/shard_map/all_gather | solution.py:10
  169.1 0.1 while.17
  169.2 0.0 copy-done.6
  169.2 0.0 copy-start.5
  169.2 0.0 copy-start.3
  169.2 3.9 subtract_reduce_fusion
  173.2 123.0 %pmax.7 = bf16[15360]{0:T(1024)(128)(2,1)S(1)} all-reduce(bf16[15360]{0:T(1024)(128)(2,1)S(1)} %subtract_reduce_fusion), channel_id=1, replica_groups=mesh['row'=32,'col'=4] {'row'}, use_global_device_ids=true, to_apply=%region_6.0 | all-reduce | flops 15360 | bytes 61440 | tf_op jit(solution)/shard_map/pmax | solution.py:70
  296.2 4.7 %exponential_reduce_fusion = bf16[15360]{0:T(1024)(128)(2,1)S(1)} fusion(f32[128,15360]{1,0:T(8,128)} %get-tuple-element.151, f32[15360]{0:T(1024)S(1)} %convert_element_type.26, f32[128]{0:T(128)S(1)} %add_subtract_fusion.1), kind=kLoop, calls=%fused_computation.8 | loop fusion | flops 5882880 | bytes 7956992 | tf_op jit(solution)/shard_map/reduce_sum | solution.py:72
  300.9 123.9 %psum.15 = bf16[15360]{0:T(1024)(128)(2,1)S(1)} all-reduce(bf16[15360]{0:T(1024)(128)(2,1)S(1)} %exponential_reduce_fusion), channel_id=1, replica_groups=mesh['row'=32,'col'=4] {'row'}, use_global_device_ids=true, to_apply=%region_8.0 | all-reduce | flops 15360 | bytes 61440 | tf_op jit(solution)/shard_map/psum | solution.py:71
  424.7 0.0 copy-done.3
  424.8 0.0 copy-done.5
  424.8 0.0 copy-start.2
  424.8 7.8 %exponential_multiply_fusion = f32[128,15360]{1,0:T(8,128)} fusion(f32[128,15360]{1,0:T(8,128)} %get-tuple-element.151, f32[15360]{0:T(1024)S(1)} %add_subtract_fusion, f32[128]{0:T(128)S(1)} %add_subtract_fusion.1), kind=kLoop, calls=%fused_computation.7 | loop fusion | flops 5898240 | bytes 15790592 | tf_op jit(solution)/shard_map/mul | solution.py:76
  432.6 0.0 copy-done.2
  (8 shorter events, 0.1 us)
Async XLA Ops:
  7.2 138.2 %copy-start = (bf16[128,128]{1,0:T(8,128)(2,1)S(1)}, bf16[128,128]{1,0:T(8,128)(2,1)}, u32[]{:S(2)}) copy-start(bf16[128,128]{1,0:T(8,128)(2,1)} %param.11) | copy-start | bytes 98308
  7.2 52.7 %all-gather.9.cloned.1.call-start = ((), (), s32[]{:S(2)}) async-start(), calls=%async_computation | async-start | bytes 4055040 | tf_op jit(solution)/shard_map/all_gather | solution.py:48
  7.9 131.2 %all-gather.11.cloned.1.call-start = ((), (), s32[]{:S(2)}) async-start(), calls=%async_computation.1 | async-start | bytes 4055040 | tf_op jit(solution)/shard_map/all_gather | solution.py:61
  66.1 8.0 %copy-start.4 = (bf16[128,128]{1,0:T(8,128)(2,1)S(1)}, bf16[128,128]{1,0:T(8,128)(2,1)}, u32[]{:S(2)}) copy-start(bf16[128,128]{1,0:T(8,128)(2,1)} %param.12) | copy-start | bytes 98308
  66.1 79.3 %copy-start.1 = (f32[15360]{0:T(1024)S(1)}, f32[15360]{0:T(1024)}, u32[]{:S(2)}) copy-start(f32[15360]{0:T(1024)} %param.17) | copy-start | bytes 184324
  145.4 23.8 %copy-start.6 = (f32[128]{0:T(128)S(1)}, f32[128]{0:T(128)}, u32[]{:S(2)}) copy-start(f32[128]{0:T(128)} %param.15) | copy-start | bytes 1540
  169.2 255.6 %copy-start.5 = (f32[128]{0:T(128)}, f32[128]{0:T(128)S(1)}, u32[]{:S(2)}) copy-start(f32[128]{0:T(128)S(1)} %add_subtract_fusion.1) | copy-start | bytes 1540
  169.2 255.5 %copy-start.3 = (f32[15360]{0:T(1024)S(1)}, f32[15360]{0:T(1024)}, u32[]{:S(2)}) copy-start(f32[15360]{0:T(1024)} %param.16) | copy-start | bytes 184324
  424.8 7.8 %copy-start.2 = (f32[15360]{0:T(1024)}, f32[15360]{0:T(1024)S(1)}, u32[]{:S(2)}) copy-start(f32[15360]{0:T(1024)S(1)} %add_subtract_fusion) | copy-start | bytes 184324
Sparse Core Ops, SparseCore 0:
  10.3 49.5 all-gather.8
  62.1 45.4 all-gather.10
where the time goes:
time: 445 us; the launch traced here: 439 us
  blocking collectives  324 us (73%)
  waiting for transfers between devices  52.5 us (12%)
  other arithmetic  21.3 us (5%)
  matrix products  15 us (3%)
  between operations  14.1 us (3%)
  local copies, waits for them, and re-layouts  12.6 us (3%)
    psum x1, blocking collectives, per_device(): lax.psum(jnp.sum(jnp.exp(col_scores - col_peak[None, :]), axis=0).astype(...  124 us
    pmax x1, blocking collectives, per_device(): col_peak = lax.pmax(for_sending(jnp.max(col_scores, axis=0)), 'row')  123 us
    psum x1, blocking collectives, per_device(): rank_core = lax.psum(partial_core_product, ('row', 'col'))  64.7 us
    all_gather x1, waiting for transfers between devices, per_device(): lax.all_gather(tgt_right, 'row', axis=0, tiled=True).astype(jnp.float32)  51.2 us
    unnamed x16, local copies, waits for them, and re-layouts  12.6 us
    all_gather x2, blocking collectives, merged(): everything = jax.tree.map(lambda part: lax.all_gather(part, axis), array)  12.2 us
  transfers between devices with their start and end apart: 2, of which 1 were waited for; matrix products, arithmetic and copies ran while one was open for 3% of the time, Pallas kernels for 0%

commit v1 on v0

v1 whole, which is shorter than its diff:
```python
import functools
import math

import jax
import jax.numpy as jnp
from jax import lax
from jax.experimental import pallas as pl
from jax.experimental.pallas import tpu as pltpu
from jax.sharding import PartitionSpec as P

MESH = pl.DeviceIdType.MESH
BF16 = jnp.bfloat16
F32 = jnp.float32
SIDE = 4
SHARE = 4
LANES = 128
REGULARIZATION = 4.0
LOG2E = math.log2(math.e)
LN2 = math.log(2.0)
SCORE = 2.0 / REGULARIZATION * LOG2E


def wrap(v):
    return lax.rem(v + 2 * SIDE, SIDE)


class Place:
    def __init__(self):
        row = lax.axis_index("row")
        self.x = lax.axis_index("col")
        self.y = lax.div(row, 2 * SIDE)
        self.z = lax.rem(lax.div(row, 2), SIDE)
        self.c = lax.rem(row, 2)

    def other(self, dx=0, dy=0, dz=0, dc=0):
        core = 1 - self.c if dc else self.c
        row = (wrap(self.y + dy) * SIDE + wrap(self.z + dz)) * 2 + core
        return {"row": row, "col": wrap(self.x + dx)}


class Gather:
    def __init__(self, here, raw, send, recv):
        self.here, self.raw, self.send, self.recv = here, raw, send, recv
        columns = raw.shape[-1]
        self.half, self.quarter = columns // 2, columns // 4
        self.copies = []

    def columns(self, kind, part):
        start = 0 if kind == "A" else self.half
        if part is None:
            return pl.ds(start, self.half)
        return pl.ds(start + part * self.quarter, self.quarter)

    def slot(self, kind, a, b, part):
        dy, dz = (a, b) if kind == "A" else (b, a)
        h = self.here
        return self.raw.at[wrap(h.y + dy), wrap(h.z + dz), h.c, :, self.columns(kind, part)]

    def target(self, kind, which, step):
        first = which == "first"
        along_z = first == (kind == "A")
        return self.here.other(dz=step) if along_z else self.here.other(dy=step)

    def copy(self, index, ref, device):
        return pltpu.make_async_remote_copy(
            src_ref=ref,
            dst_ref=ref,
            send_sem=self.send.at[index],
            recv_sem=self.recv.at[index],
            device_id=device,
            device_id_type=MESH,
        )

    def start(self, kind, number, a, b, part, which, step):
        base = 0 if kind == "A" else 24
        device = self.target(kind, which, step)
        copy = self.copy(base + number, self.slot(kind, a, b, part), device)
        copy.start()
        self.copies.append(copy)

    def arrived(self, kind, number, a, b, part):
        base = 0 if kind == "A" else 24
        copy = self.copy(base + number, self.slot(kind, a, b, part), self.here.other(dc=1))
        copy.wait_recv()

    def line(self, kind, number, a):
        h = self.here
        if kind == "A":
            ref = self.raw.at[wrap(h.y + a), :, h.c, :, self.columns(kind, None)]
        else:
            ref = self.raw.at[:, wrap(h.z + a), h.c, :, self.columns(kind, None)]
        base = 0 if kind == "A" else 24
        copy = self.copy(base + 20 + number, ref, h.other(dc=1))
        copy.start()
        self.copies.append(copy)

    def own(self):
        for kind in "AB":
            self.start(kind, 0, 0, 0, None, "first", 1)
            self.start(kind, 1, 0, 0, None, "first", -1)
        for kind in "AB":
            self.start(kind, 2, 0, 0, None, "last", 1)
            self.start(kind, 3, 0, 0, None, "last", -1)

    def first(self):
        for kind in "AB":
            self.arrived(kind, 0, 0, -1, None)
            self.start(kind, 4, 0, -1, 0, "first", 1)
            self.start(kind, 6, 0, -1, None, "last", 1)
            self.start(kind, 7, 0, -1, None, "last", -1)
            self.arrived(kind, 1, 0, 1, None)
            self.start(kind, 5, 0, 1, 1, "first", -1)
            self.start(kind, 8, 0, 1, None, "last", 1)
            self.start(kind, 9, 0, 1, None, "last", -1)

    def first_last(self):
        for kind in "AB":
            self.arrived(kind, 2, -1, 0, None)
            self.start(kind, 12, -1, 0, 0, "last", 1)
            self.arrived(kind, 3, 1, 0, None)
            self.start(kind, 16, 1, 0, 1, "last", -1)

    def second(self):
        for kind in "AB":
            self.arrived(kind, 4, 0, 2, 0)
            self.arrived(kind, 5, 0, 2, 1)
            self.start(kind, 10, 0, 2, None, "last", 1)
            self.start(kind, 11, 0, 2, None, "last", -1)
            self.line(kind, 0, 0)

    def second_last(self):
        for kind in "AB":
            for k, b in ((0, -1), (1, 1)):
                self.arrived(kind, 6 + 2 * k, -1, b, None)
                self.start(kind, 13 + k, -1, b, 0, "last", 1)
                self.arrived(kind, 7 + 2 * k, 1, b, None)
                self.start(kind, 17 + k, 1, b, 1, "last", -1)

    def third(self):
        for kind in "AB":
            self.arrived(kind, 10, -1, 2, None)
            self.start(kind, 15, -1, 2, 0, "last", 1)
            self.line(kind, 1, -1)
            self.arrived(kind, 11, 1, 2, None)
            self.start(kind, 19, 1, 2, 1, "last", -1)
            self.line(kind, 2, 1)

    def fourth(self):
        for kind in "AB":
            for k, b in enumerate((0, -1, 1, 2)):
                self.arrived(kind, 12 + k, 2, b, 0)
                self.arrived(kind, 16 + k, 2, b, 1)
            self.line(kind, 3, 2)

    def siblings(self):
        h = self.here
        for kind in "AB":
            base = 0 if kind == "A" else 24
            for number, a in enumerate((0, -1, 1, 2)):
                if kind == "A":
                    ref = self.raw.at[wrap(h.y + a), :, 1 - h.c, :, self.columns(kind, None)]
                else:
                    ref = self.raw.at[:, wrap(h.z + a), 1 - h.c, :, self.columns(kind, None)]
                self.copy(base + 20 + number, ref, h.other(dc=1)).wait_recv()

    def finish(self):
        for copy in self.copies:
            copy.wait_send()


class Exchange:
    def __init__(self, here, buffer, send, recv, axis):
        self.here, self.buffer, self.send, self.recv, self.axis = here, buffer, send, recv, axis
        self.me = getattr(here, axis)

    def copies(self):
        for k, step in enumerate((1, -1, 2)):
            ref = self.buffer.at[self.me]
            yield pltpu.make_async_remote_copy(
                src_ref=ref,
                dst_ref=ref,
                send_sem=self.send.at[k],
                recv_sem=self.recv.at[k],
                device_id=self.here.other(**{"d" + self.axis: step}),
                device_id_type=MESH,
            )

    def start(self):
        for copy in self.copies():
            copy.start()

    def wait(self):
        for k, step in enumerate((1, -1, 2)):
            ref = self.buffer.at[wrap(self.me - step)]
            pltpu.make_async_remote_copy(
                src_ref=ref,
                dst_ref=ref,
                send_sem=self.send.at[k],
                recv_sem=self.recv.at[k],
                device_id=self.here.other(dc=1),
                device_id_type=MESH,
            ).wait_recv()

    def finish(self):
        for copy in self.copies():
            copy.wait_send()


def to_sibling(here, src, dst, send, recv, index):
    return pltpu.make_async_remote_copy(
        src_ref=src,
        dst_ref=dst,
        send_sem=send.at[index],
        recv_sem=recv.at[index],
        device_id=here.other(dc=1),
        device_id_type=MESH,
    )


def added(parts):
    return (parts[0] + parts[1]) + (parts[2] + parts[3])


def merged(parts):
    peak = functools.reduce(jnp.maximum, parts)
    total = functools.reduce(jnp.add, [jnp.exp2(part - peak) for part in parts])
    return peak + jnp.log2(total)


def step_of(columns, most):
    return max(s for s in range(LANES, most + 1, LANES) if columns % s == 0)


def main_kernel(
    coupling_hbm, tgt_right_hbm, tgt_left_hbm,
    src_left, src_right, log_src, log_tgt, tgt_potential,
    left_out, rows_out, row_shift_out, row_out, col_out,
    raw_right, raw_left, wide, image, whole_left, core_part, core_sib, core_x, core_y, core_z, core_half,
    peaks, totals, row_parts, col_all, col_sib, col_z, col_y, image_acc,
    local, right_send, right_recv, left_send, left_recv,
    small_send, small_recv, sib_send, sib_recv,
):
    here = Place()
    columns = wide.shape[1]
    rows = wide.shape[0]

    own_right = pltpu.make_async_copy(tgt_right_hbm, raw_right.at[here.y, here.z, here.c], local.at[0])
    own_left = pltpu.make_async_copy(tgt_left_hbm, raw_left.at[here.y, here.z, here.c], local.at[1])
    own_right.start()
    own_left.start()
    load = pltpu.make_async_copy(coupling_hbm, wide, local.at[2])
    load.start()

    barrier = pltpu.get_barrier_semaphore()
    partners = [here.other(dc=1)]
    for axis in "xyz":
        partners += [here.other(**{"d" + axis: step}) for step in (1, -1, 2)]
    for partner in partners:
        pl.semaphore_signal(barrier, inc=1, device_id=partner, device_id_type=MESH)
    own_right.wait()
    own_left.wait()
    pl.semaphore_wait(barrier, len(partners))

    right = Gather(here, raw_right, right_send, right_recv)
    left = Gather(here, raw_left, left_send, left_recv)
    right.own()

    side = src_right[...].astype(F32).T.astype(BF16)
    width = step_of(columns, 512)

    def image_step(i, _):
        at = pl.ds(pl.multiple_of(i * width, width), width)
        entries = wide[:, at]
        high = entries.astype(BF16)
        low = (entries - high.astype(F32)).astype(BF16)
        value = jnp.dot(side, high, preferred_element_type=F32) + jnp.dot(side, low, preferred_element_type=F32)
        value_high = value.astype(BF16)
        image[0:rows, at] = value_high
        image[rows : 2 * rows, at] = (value - value_high.astype(F32)).astype(BF16)
        return 0

    steps = columns // width
    cut_one, cut_two = steps // 4, (steps * 5) // 8
    load.wait()
    lax.fori_loop(0, cut_one, image_step, 0)
    right.first()
    right.first_last()
    left.own()
    lax.fori_loop(cut_one, cut_two, image_step, 0)
    right.second()
    lax.fori_loop(cut_two, steps, image_step, 0)
    right.second_last()
    right.third()
    left.first()
    left.first_last()
    right.fourth()
    right.siblings()

    image_acc[...] = jnp.zeros_like(image_acc)
    span = step_of(columns, 3072)

    def core_step(i, _):
        at = pl.ds(pl.multiple_of(i * span, span), span)
        factor = raw_right[:, :, :, :, at].reshape(LANES, span)
        image_acc[...] += lax.dot_general(
            image[:, at], factor, (((1,), (1,)), ((), ())), preferred_element_type=F32
        )
        return 0

    lax.fori_loop(0, columns // span, core_step, 0)
    core_part[...] = image_acc[0:LANES] + image_acc[LANES : 2 * LANES]

    part_rows = LANES // 2
    mine = pl.ds(pl.multiple_of(here.c * part_rows, part_rows), part_rows)
    theirs = pl.ds(pl.multiple_of((1 - here.c) * part_rows, part_rows), part_rows)
    core_swap = to_sibling(here, core_part.at[theirs], core_sib, sib_send, sib_recv, 0)
    core_swap.start()
    left.second()
    core_swap.wait_recv()
    core_x[here.x] = core_part[mine] + core_sib[...]
    sum_x = Exchange(here, core_x, small_send.at[0], small_recv.at[0], "x")
    sum_x.start()
    left.second_last()
    sum_x.wait()
    core_y[here.y] = added([core_x[k] for k in range(SIDE)])
    sum_y = Exchange(here, core_y, small_send.at[1], small_recv.at[1], "y")
    sum_y.start()
    left.third()
    sum_y.wait()
    core_z[here.z] = added([core_y[k] for k in range(SIDE)])
    sum_z = Exchange(here, core_z, small_send.at[2], small_recv.at[2], "z")
    sum_z.start()
    left.fourth()
    sum_z.wait()
    core_half[here.c] = added([core_z[k] for k in range(SIDE)]).astype(BF16)
    half_swap = to_sibling(here, core_half.at[here.c], core_half.at[here.c], sib_send, sib_recv, 1)
    half_swap.start()
    to_sibling(here, core_half.at[1 - here.c], core_half.at[1 - here.c], sib_send, sib_recv, 1).wait_recv()
    core = core_half[...].reshape(LANES, LANES)
    rows_cost = jnp.dot(src_left[...], core, preferred_element_type=F32).astype(BF16)
    rows_out[...] = rows_cost
    left.siblings()

    peaks[...] = jnp.full_like(peaks, -jnp.inf)
    reach = step_of(columns, 1024)
    tiles = reach // LANES

    def score_step(i, _):
        at = pl.ds(pl.multiple_of(i * reach, reach), reach)
        factor = raw_left[:, :, :, :, at].reshape(LANES, reach)
        whole_left[:, at] = factor
        score = jnp.dot(rows_out[...], factor, preferred_element_type=F32) * SCORE
        wide[:, at] = score
        peak = peaks[...]
        for q in range(tiles):
            shift = tgt_potential[pl.ds(i * tiles + q, 1), :] * LOG2E
            peak = jnp.maximum(peak, score[:, q * LANES : (q + 1) * LANES] + shift)
        peaks[...] = peak
        return 0

    lax.fori_loop(0, columns // reach, score_step, 0)
    save = pltpu.make_async_copy(whole_left, left_out, local.at[3])
    save.start()

    totals[...] = jnp.zeros_like(totals)

    def total_step(i, _):
        peak = peaks[...]
        total = totals[...]
        for q in range(tiles):
            at = pl.ds(pl.multiple_of(i * reach + q * LANES, LANES), LANES)
            shift = tgt_potential[pl.ds(i * tiles + q, 1), :] * LOG2E
            total = total + jnp.exp2(wide[:, at] + shift - peak)
        totals[...] = total
        return 0

    lax.fori_loop(0, columns // reach, total_step, 0)
    lane_peak = peaks[...].T
    row_peak = jnp.max(lane_peak, axis=0, keepdims=True)
    row_total = jnp.sum(totals[...].T * jnp.exp2(lane_peak - row_peak), axis=0, keepdims=True)
    row_parts[here.x] = jnp.broadcast_to(row_peak + jnp.log2(row_total), row_parts.shape[1:])
    rows_x = Exchange(here, row_parts, small_send.at[3], small_recv.at[3], "x")
    rows_x.start()
    rows_x.wait()
    row_sum = merged([row_parts[k] for k in range(SIDE)])[0:1]
    row_potential = log_src[...] - LN2 * row_sum
    row_out[...] = row_potential
    row_shift_out[...] = jnp.broadcast_to(row_potential * LOG2E, (LANES, LANES)).T

    def col_step(i, _):
        shift = row_shift_out[...]
        for q in range(tiles):
            at = pl.ds(pl.multiple_of(i * reach + q * LANES, LANES), LANES)
            score = wide[:, at] + shift
            peak = jnp.max(score, axis=0, keepdims=True)
            total = jnp.sum(jnp.exp2(score - peak), axis=0, keepdims=True)
            col_all[pl.ds(i * tiles + q, 1), :] = peak + jnp.log2(total)
        return 0

    lax.fori_loop(0, columns // reach, col_step, 0)

    col_rows = col_all.shape[0]
    some = col_sib.shape[0]
    rest = col_rows - some
    mine = pl.ds(pl.multiple_of(here.c * rest, 8), some)
    theirs = pl.ds(pl.multiple_of((1 - here.c) * rest, 8), some)
    col_swap = to_sibling(here, col_all.at[theirs], col_sib, sib_send, sib_recv, 2)
    col_swap.start()
    col_swap.wait_recv()
    col_z[here.z] = merged([col_all[mine, :], col_sib[...]])
    sum_z2 = Exchange(here, col_z, small_send.at[4], small_recv.at[4], "z")
    sum_z2.start()
    sum_z2.wait()
    col_y[here.y] = merged([col_z[k] for k in range(SIDE)])
    sum_y2 = Exchange(here, col_y, small_send.at[5], small_recv.at[5], "y")
    sum_y2.start()
    sum_y2.wait()
    col_out[mine, :] = log_tgt[mine, :] - LN2 * merged([col_y[k] for k in range(SIDE)])
    sent = pl.ds(pl.multiple_of(here.c * some, 8), rest)
    taken = pl.ds(pl.multiple_of((1 - here.c) * some, 8), rest)
    col_share = to_sibling(here, col_out.at[sent], col_out.at[sent], sib_send, sib_recv, 3)
    col_share.start()
    to_sibling(here, col_out.at[taken], col_out.at[taken], sib_send, sib_recv, 3).wait_recv()

    save.wait()
    right.finish()
    left.finish()
    for exchange in (sum_x, sum_y, sum_z, rows_x, sum_z2, sum_y2):
        exchange.finish()
    for copy in (core_swap, half_swap, col_swap, col_share):
        copy.wait_send()


def plan_kernel(source_count, rows_cost, row_shift, row_in, col_in, left, plan, row_out, col_out):
    i = pl.program_id(0)
    row_out[...] = row_in[...]
    tiles = plan.shape[1] // LANES
    score = jnp.dot(rows_cost[...], left[...], preferred_element_type=F32) * SCORE
    shift = row_shift[...]
    for q in range(tiles):
        here = pl.ds(i * tiles + q, 1)
        potential = col_in[here, :]
        col_out[here, :] = potential
        part = score[:, q * LANES : (q + 1) * LANES] + shift
        plan[:, q * LANES : (q + 1) * LANES] = jnp.exp2(part + (potential * LOG2E + math.log2(source_count)))


def per_device(
    coupling,
    src_left,
    emitter_distance_rightside,
    destination_distance_leftside,
    tgt_right,
    log_src,
    logarithm_destination_masses,
    tgt_potential,
):
    rows, columns = coupling.shape
    rank = src_left.shape[1]
    col_rows = columns // LANES
    some = -(-col_rows // 16) * 8
    source_count = rows * lax.axis_size("row")
    blocks = (SIDE, SIDE, 2, SHARE, columns)
    vmem = pl.BlockSpec(memory_space=pltpu.VMEM)
    anywhere = pl.BlockSpec(memory_space=pl.ANY)
    left, rows_cost, row_shift, row_potential, col_potential = pl.pallas_call(
        main_kernel,
        name="main",
        out_shape=[
            jax.ShapeDtypeStruct((rank, columns), BF16),
            jax.ShapeDtypeStruct((rows, rank), BF16),
            jax.ShapeDtypeStruct((rows, LANES), F32),
            jax.ShapeDtypeStruct((1, rows), F32),
            jax.ShapeDtypeStruct((col_rows, LANES), F32),
        ],
        in_specs=[anywhere] * 3 + [vmem] * 5,
        out_specs=[anywhere] + [vmem] * 4,
        scratch_shapes=[
            pltpu.VMEM(blocks, BF16),
            pltpu.VMEM(blocks, BF16),
            pltpu.VMEM((rows, columns), F32),
            pltpu.VMEM((2 * rank, columns), BF16),
            pltpu.VMEM((rank, columns), BF16),
            pltpu.VMEM((rank, rank), F32),
            pltpu.VMEM((rank // 2, rank), F32),
            pltpu.VMEM((SIDE, rank // 2, rank), F32),
            pltpu.VMEM((SIDE, rank // 2, rank), F32),
            pltpu.VMEM((SIDE, rank // 2, rank), F32),
            pltpu.VMEM((2, rank // 2, rank), BF16),
            pltpu.VMEM((rows, LANES), F32),
            pltpu.VMEM((rows, LANES), F32),
            pltpu.VMEM((SIDE, 8, LANES), F32),
            pltpu.VMEM((col_rows, LANES), F32),
            pltpu.VMEM((some, LANES), F32),
            pltpu.VMEM((SIDE, some, LANES), F32),
            pltpu.VMEM((SIDE, some, LANES), F32),
            pltpu.VMEM((2 * rank, rank), F32),
            pltpu.SemaphoreType.DMA((4,)),
            pltpu.SemaphoreType.DMA((48,)),
            pltpu.SemaphoreType.DMA((48,)),
            pltpu.SemaphoreType.DMA((48,)),
            pltpu.SemaphoreType.DMA((48,)),
            pltpu.SemaphoreType.DMA((6, 3)),
            pltpu.SemaphoreType.DMA((6, 3)),
            pltpu.SemaphoreType.DMA((4,)),
            pltpu.SemaphoreType.DMA((4,)),
        ],
        compiler_params=pltpu.CompilerParams(
            collective_id=0, has_side_effects=True, vmem_limit_bytes=56 * 1024 * 1024
        ),
    )(
        coupling,
        tgt_right,
        destination_distance_leftside,
        src_left,
        emitter_distance_rightside,
        log_src.reshape(1, rows),
        logarithm_destination_masses.reshape(col_rows, LANES),
        tgt_potential.reshape(col_rows, LANES),
    )
    width = step_of(columns, 1536)
    whole = lambda *shape: pl.BlockSpec(shape, lambda i: (0,) * len(shape))
    plan, row_potential, col_potential = pl.pallas_call(
        functools.partial(plan_kernel, source_count),
        name="plan",
        grid=(columns // width,),
        out_shape=[
            jax.ShapeDtypeStruct((rows, columns), F32),
            jax.ShapeDtypeStruct((1, rows), F32),
            jax.ShapeDtypeStruct((col_rows, LANES), F32),
        ],
        in_specs=[
            whole(rows, rank),
            whole(rows, LANES),
            whole(1, rows),
            whole(col_rows, LANES),
            pl.BlockSpec((rank, width), lambda i: (0, i)),
        ],
        out_specs=[pl.BlockSpec((rows, width), lambda i: (0, i)), whole(1, rows), whole(col_rows, LANES)],
        compiler_params=pltpu.CompilerParams(vmem_limit_bytes=32 * 1024 * 1024),
    )(rows_cost, row_shift, row_potential, col_potential, left)
    return plan, row_potential.reshape(rows), col_potential.reshape(columns)


def solution(mesh):
    return jax.shard_map(
        per_device,
        mesh=mesh,
        in_specs=(
            P("row", "col"),
            P("row", None),
            P("row", None),
            P("row", "col"),
            P("row", "col"),
            P("row"),
            P("col"),
            P("col"),
        ),
        out_specs=(P("row", "col"), P("row"), P("col")),
        check_vma=False,
    )
```

time: 445 us -> 80.7 us (0.18); the launches traced: 439 us -> 80.3 us
  blocking collectives: 324 us -> 0 us
  Pallas kernels: 0 us -> 74.5 us
  waiting for transfers between devices: 52.5 us -> 0 us
  other arithmetic: 21.3 us -> 0 us
  matrix products: 15 us -> 0 us
  between operations: 14.1 us -> 0.65 us
  local copies, waits for them, and re-layouts: 12.6 us -> 5.16 us
    psum x2 -> x0, blocking collectives: 189 us -> none  [the longest x1 124 us: per_device(): lax.psum(jnp.sum(jnp.exp(col_scores - col_peak[None, :]), axis=0).astype(...]
    pmax x1 -> x0, blocking collectives: 123 us -> none  [per_device(): col_peak = lax.pmax(for_sending(jnp.max(col_scores, axis=0)), 'row')]
    pallas_call x0 -> x2, Pallas kernels: none -> 74.5 us  [the longest x1 68.3 us: per_device(): pl.pallas_call(main_kernel, name='main', out_shape=[jax.ShapeDtypeStruct(...]
    all_gather x2 -> x0, waiting for transfers between devices: 51.2 us -> none  [the longest x1 51.2 us: per_device(): lax.all_gather(tgt_right, 'row', axis=0, tiled=True).astype(jnp.float32)]
    dot_general x3 -> x0, matrix products: 15 us -> none  [the longest x1 8.03 us: per_device(): lax.dot_general(coupling, lax.all_gather(tgt_right, 'row', axis=0, tiled=...]
    all_gather x2 -> x0, blocking collectives: 12.2 us -> none  [merged(): everything = jax.tree.map(lambda part: lax.all_gather(part, axis), array)]
    reduce_sum x2 -> x0, other arithmetic: 9.41 us -> none  [the longest x1 4.73 us: per_device(): row_total = jnp.sum(jnp.exp(row_scores - row_peak[:, None]), axis=1)]
    mul x1 -> x0, other arithmetic: 7.83 us -> none  [per_device(): source_count * jnp.exp(row_potential[:, None] + col_potential[None, :] -...]
  transfers between devices with their start and end apart: 2 -> 0, of which waited for: 1 -> 0; matrix products, arithmetic and copies ran while one was open for 3% -> 0% of each run, Pallas kernels for 0% -> 0%
where the time goes in v1:
time: 80.7 us; the launch traced here: 80.3 us
  Pallas kernels  74.5 us (92%)
  local copies, waits for them, and re-layouts  5.16 us (6%)
    pallas_call x1, Pallas kernels, per_device(): pl.pallas_call(main_kernel, name='main', out_shape=[jax.ShapeDtypeStruct(...  68.3 us
    pallas_call x1, Pallas kernels, per_device(): pl.pallas_call(functools.partial(plan_kernel, source_count), name='plan',...  6.16 us
    unnamed x10, local copies, waits for them, and re-layouts  5.16 us

profile of v1, /device:TPU:1, one launch (start us, length us, event | category | flops | bytes accessed | tf_op | source)
XLA Modules:
  0.0 80.3 jit_solution(13502252959617747693)
XLA Ops:
  0.6 68.3 %main.1 = (bf16[128,15360]{1,0:T(8,128)(2,1)}, bf16[128,128]{1,0:T(8,128)(2,1)}, f32[128,128]{1,0:T(8,128)}, f32[1,128]{1,0:T(1,128)}, f32[120,128]{1,0:T(8,128)}) custom-call(f32[128,15360]{1,0:T(8,128)} %coupling_hbm.1, bf16[4,15360]{1,0:T(4,128)(2,1)} %tgt_right_hbm.1, bf16[4,15360]{1,0:T(4,128)(2,1)} %tgt_left_hbm.1, bf16[128,128]{1,0:T(8,128)(2,1)} %src_left.1, ...), custom_call_target="tpu_custom_call" | custom-call | tf_op jit(solution)/shard_map/main/pallas_call | solution.py:466
  69.0 0.0 copy-start
  69.0 2.1 %copy-done = bf16[128,15360]{1,0:T(8,128)(2,1)S(1)} copy-done((bf16[128,15360]{1,0:T(8,128)(2,1)S(1)}, bf16[128,15360]{1,0:T(8,128)(2,1)}, u32[]{:S(2)}) %copy-start) | copy-done | bytes 3932184
  71.1 0.0 copy-start.1
  71.1 0.8 %copy-done.1 = f32[128,128]{1,0:T(8,128)S(1)} copy-done((f32[128,128]{1,0:T(8,128)S(1)}, f32[128,128]{1,0:T(8,128)}, u32[]{:S(2)}) %copy-start.1) | copy-done | bytes 65560
  71.9 0.0 copy-start.2
  71.9 0.8 %copy-done.2 = f32[120,128]{1,0:T(8,128)S(1)} copy-done((f32[120,128]{1,0:T(8,128)S(1)}, f32[120,128]{1,0:T(8,128)}, u32[]{:S(2)}) %copy-start.2) | copy-done | bytes 61464
  72.7 0.0 copy-start.3
  72.7 0.8 copy-done.3
  73.5 0.0 copy-start.4
  73.5 0.6 copy-done.4
  74.1 6.2 %plan.1 = (f32[128,15360]{1,0:T(8,128)}, f32[1,128]{1,0:T(1,128)}, f32[120,128]{1,0:T(8,128)}) custom-call(bf16[128,128]{1,0:T(8,128)(2,1)S(1)} %copy-done.3, f32[128,128]{1,0:T(8,128)S(1)} %copy-done.1, f32[1,128]{1,0:T(1,128)S(1)} %copy-done.4, f32[120,128]{1,0:T(8,128)S(1)} %copy-done.2, bf16[128,15360]{1,0:T(8,128)(2,1)S(1)} %copy-done), custom_call_target="tpu_custom_call" | custom-call | tf_op jit(solution)/shard_map/plan/pallas_call | solution.py:523
Async XLA Ops:
  69.0 2.1 %copy-start = (bf16[128,15360]{1,0:T(8,128)(2,1)S(1)}, bf16[128,15360]{1,0:T(8,128)(2,1)}, u32[]{:S(2)}) copy-start(bf16[128,15360]{1,0:T(8,128)(2,1)} %get-tuple-element.15.left) | copy-start | bytes 11796484
  71.1 0.8 %copy-start.1 = (f32[128,128]{1,0:T(8,128)S(1)}, f32[128,128]{1,0:T(8,128)}, u32[]{:S(2)}) copy-start(f32[128,128]{1,0:T(8,128)} %get-tuple-element.12.row_shift) | copy-start | bytes 196612
  71.9 0.8 %copy-start.2 = (f32[120,128]{1,0:T(8,128)S(1)}, f32[120,128]{1,0:T(8,128)}, u32[]{:S(2)}) copy-start(f32[120,128]{1,0:T(8,128)} %get-tuple-element.14.col_in) | copy-start | bytes 184324
  72.7 0.8 copy-start.3
  73.5 0.6 copy-start.4

commit v2 on v1

v2 whole, which is shorter than its diff:
```python
import functools
import math

import jax
import jax.numpy as jnp
from jax import lax
from jax.experimental import pallas as pl
from jax.experimental.pallas import tpu as pltpu
from jax.sharding import PartitionSpec as P

MESH = pl.DeviceIdType.MESH
BF16 = jnp.bfloat16
F32 = jnp.float32
SIDE = 4
SHARE = 4
LANES = 128
REGULARIZATION = 4.0
LOG2E = math.log2(math.e)
LN2 = math.log(2.0)
SCORE = 2.0 / REGULARIZATION * LOG2E


def wrap(v):
    return lax.rem(v + 2 * SIDE, SIDE)


class Place:
    def __init__(self):
        row = lax.axis_index("row")
        self.x = lax.axis_index("col")
        self.y = lax.div(row, 2 * SIDE)
        self.z = lax.rem(lax.div(row, 2), SIDE)
        self.c = lax.rem(row, 2)

    def other(self, dx=0, dy=0, dz=0, dc=0):
        core = 1 - self.c if dc else self.c
        row = (wrap(self.y + dy) * SIDE + wrap(self.z + dz)) * 2 + core
        return {"row": row, "col": wrap(self.x + dx)}


class Gather:
    KINDS = ("A", "B")
    MESSAGES = 37

    def __init__(self, here, raw, send, recv):
        self.here, self.raw, self.send, self.recv = here, raw, send, recv
        columns = raw.shape[-1]
        self.half, self.quarter = columns // 2, columns // 4
        self.started = []

    def ref(self, kind, a, b, part, core=None):
        h = self.here
        core = h.c if core is None else core
        start = 0 if kind == "A" else self.half
        if part is None:
            columns = pl.ds(start, self.half)
        else:
            columns = pl.ds(start + part * self.quarter, self.quarter)
        dy, dz = (a, b) if kind == "A" else (b, a)
        y = slice(None) if dy is None else wrap(h.y + dy)
        z = slice(None) if dz is None else wrap(h.z + dz)
        return self.raw.at[y, z, core, :, columns]

    def copy(self, kind, number, ref, device):
        index = number + (0 if kind == "A" else self.MESSAGES)
        return pltpu.make_async_remote_copy(
            src_ref=ref,
            dst_ref=ref,
            send_sem=self.send.at[index],
            recv_sem=self.recv.at[index],
            device_id=device,
            device_id_type=MESH,
        )

    def start(self, kind, number, ref, device):
        copy = self.copy(kind, number, ref, device)
        copy.start()
        self.started.append(copy)

    def wait(self, kind, number, ref):
        self.copy(kind, number, ref, self.here.other(dc=1)).wait_recv()

    def along(self, kind, first, step):
        if first == (kind == "A"):
            return self.here.other(dz=step)
        return self.here.other(dy=step)


    @staticmethod
    def side(step):
        return 0 if step == 1 else 1

    def first_number(self, part, step):
        return part * 2 + self.side(step)

    def last_number(self, b, part, step):
        return 6 + (b + 1) * 4 + part * 2 + self.side(step)

    def on_number(self, b, step):
        return 22 + (b + 1) * 2 + self.side(step)

    def first(self, kind, part, step):
        self.start(kind, self.first_number(part, step), self.ref(kind, 0, 0, part), self.along(kind, True, step))

    def wait_first(self, kind, part, step):
        self.wait(kind, self.first_number(part, step), self.ref(kind, 0, -step, part))

    def first_on(self, kind, step):
        part = self.side(step)
        self.start(kind, 4 + part, self.ref(kind, 0, -step, part), self.along(kind, True, step))

    def wait_first_on(self, kind, step):
        part = self.side(step)
        self.wait(kind, 4 + part, self.ref(kind, 0, 2, part))

    def last(self, kind, b, part, step):
        self.start(kind, self.last_number(b, part, step), self.ref(kind, 0, b, part), self.along(kind, False, step))

    def wait_last(self, kind, b, part, step):
        self.wait(kind, self.last_number(b, part, step), self.ref(kind, -step, b, part))

    def last_on(self, kind, b, step):
        part = self.side(step)
        self.start(kind, self.on_number(b, step), self.ref(kind, -step, b, part), self.along(kind, False, step))

    def wait_last_on(self, kind, b, step):
        part = self.side(step)
        self.wait(kind, self.on_number(b, step), self.ref(kind, 2, b, part))

    def to_sibling(self, kind, number, a, b):
        self.start(kind, 30 + number, self.ref(kind, a, b, None), self.here.other(dc=1))

    def wait_sibling(self, kind, number, a, b):
        self.wait(kind, 30 + number, self.ref(kind, a, b, None, 1 - self.here.c))

    STEPS = ((1, 0), (-1, 1))

    def step(self, number):
        getattr(self, "step_%d" % number)()

    def step_0(self):
        for kind in self.KINDS:
            for step, part in self.STEPS:
                self.first(kind, part, step)
        for kind in self.KINDS:
            for step, part in self.STEPS:
                self.first(kind, 1 - part, step)
        for kind in self.KINDS:
            for step, part in self.STEPS:
                self.last(kind, 0, part, step)
        for kind in self.KINDS:
            for step, part in self.STEPS:
                self.last(kind, 0, 1 - part, step)

    def step_1(self):
        for kind in self.KINDS:
            for step, part in self.STEPS:
                self.wait_first(kind, part, step)
                self.first_on(kind, step)
                self.last(kind, -step, part, step)

    def step_2(self):
        for kind in self.KINDS:
            for step, part in self.STEPS:
                self.wait_first(kind, 1 - part, step)
                self.last(kind, -step, 1 - part, -step)

    def step_3(self):
        for kind in self.KINDS:
            for step, part in self.STEPS:
                self.wait_last(kind, 0, part, step)
                self.last_on(kind, 0, step)
        for kind in self.KINDS:
            for b in (-1, 1):
                for step, part in self.STEPS:
                    self.last(kind, b, 1 - part, step)

    def step_4(self):
        for kind in self.KINDS:
            for step, part in self.STEPS:
                self.wait_first_on(kind, step)
                self.last(kind, 2, part, step)
        for kind in self.KINDS:
            self.to_sibling(kind, 0, 0, None)

    def step_5(self):
        for kind in self.KINDS:
            for b in (-1, 1):
                for step, part in self.STEPS:
                    self.wait_last(kind, b, part, step)
                    self.last_on(kind, b, step)
        for kind in self.KINDS:
            for step, part in self.STEPS:
                self.last(kind, 2, 1 - part, step)

    def step_6(self):
        for kind in self.KINDS:
            for step, part in self.STEPS:
                self.wait_last(kind, 2, part, step)
                self.last_on(kind, 2, step)

    def step_7(self):
        for kind in self.KINDS:
            for step, part in self.STEPS:
                for b in (0, -1, 1, 2):
                    self.wait_last(kind, b, 1 - part, step)
                self.to_sibling(kind, 1 + part, -step, None)

    def step_8(self):
        for k, b in enumerate((0, -1, 1, 2)):
            for kind in self.KINDS:
                for step, part in self.STEPS:
                    self.wait_last_on(kind, b, step)
                self.to_sibling(kind, 3 + k, 2, b)

    def step_9(self):
        for kind in self.KINDS:
            for k, a in enumerate((0, -1, 1)):
                self.wait_sibling(kind, k, a, None)
            for k, b in enumerate((0, -1, 1, 2)):
                self.wait_sibling(kind, 3 + k, 2, b)

    def finish(self):
        for copy in self.started:
            copy.wait_send()


class Exchange:
    def __init__(self, here, buffer, send, recv, axis):
        self.here, self.buffer, self.send, self.recv, self.axis = here, buffer, send, recv, axis
        self.me = getattr(here, axis)

    def copies(self):
        for k, step in enumerate((1, -1, 2)):
            ref = self.buffer.at[self.me]
            yield pltpu.make_async_remote_copy(
                src_ref=ref,
                dst_ref=ref,
                send_sem=self.send.at[k],
                recv_sem=self.recv.at[k],
                device_id=self.here.other(**{"d" + self.axis: step}),
                device_id_type=MESH,
            )

    def start(self):
        for copy in self.copies():
            copy.start()

    def wait(self):
        for k, step in enumerate((1, -1, 2)):
            ref = self.buffer.at[wrap(self.me - step)]
            pltpu.make_async_remote_copy(
                src_ref=ref,
                dst_ref=ref,
                send_sem=self.send.at[k],
                recv_sem=self.recv.at[k],
                device_id=self.here.other(dc=1),
                device_id_type=MESH,
            ).wait_recv()

    def finish(self):
        for copy in self.copies():
            copy.wait_send()


def to_sibling(here, src, dst, send, recv, index):
    return pltpu.make_async_remote_copy(
        src_ref=src,
        dst_ref=dst,
        send_sem=send.at[index],
        recv_sem=recv.at[index],
        device_id=here.other(dc=1),
        device_id_type=MESH,
    )


def added(parts):
    return (parts[0] + parts[1]) + (parts[2] + parts[3])


def merged(parts):
    peak = functools.reduce(jnp.maximum, parts)
    total = functools.reduce(jnp.add, [jnp.exp2(part - peak) for part in parts])
    return peak + jnp.log2(total)


def step_of(columns, most):
    return max(s for s in range(LANES, most + 1, LANES) if columns % s == 0)


def main_kernel(
    coupling_hbm, tgt_right_hbm, tgt_left_hbm,
    src_left_hbm, src_right_hbm, log_src_hbm, log_tgt_hbm, tgt_potential_hbm,
    wide, row_shift_out, row_out, col_out,
    raw_right, raw_left, image, core_part, core_sib, core_x, core_y, core_z, core_half,
    peaks, totals, row_parts, col_all, col_sib, col_z, col_y, image_acc,
    src_left, src_right, log_src, log_tgt, tgt_potential,
    local, right_send, right_recv, left_send, left_recv,
    small_send, small_recv, sib_send, sib_recv,
):
    here = Place()
    columns = wide.shape[1]
    rows = wide.shape[0]

    loads = []
    for k, (source, target) in enumerate((
        (tgt_right_hbm, raw_right.at[here.y, here.z, here.c]),
        (src_right_hbm, src_right),
        (tgt_left_hbm, raw_left.at[here.y, here.z, here.c]),
        (coupling_hbm, wide),
        (src_left_hbm, src_left),
        (log_src_hbm, log_src),
        (log_tgt_hbm, log_tgt),
        (tgt_potential_hbm, tgt_potential),
    )):
        loads.append(pltpu.make_async_copy(source, target, local.at[k]))
        loads[-1].start()

    barrier = pltpu.get_barrier_semaphore()
    partners = [here.other(dc=1)]
    for axis in "xyz":
        partners += [here.other(**{"d" + axis: step}) for step in (1, -1, 2)]
    for partner in partners:
        pl.semaphore_signal(barrier, inc=1, device_id=partner, device_id_type=MESH)
    loads[0].wait()
    pl.semaphore_wait(barrier, len(partners))

    right = Gather(here, raw_right, right_send, right_recv)
    left = Gather(here, raw_left, left_send, left_recv)
    right.step(0)

    for k in (1, 2, 3):
        loads[k].wait()
    side = src_right[...].astype(F32).T.astype(BF16)
    side = jnp.concatenate([side, side], axis=1)
    width = step_of(columns, 3072)

    def image_step(i, _):
        at = pl.ds(pl.multiple_of(i * width, width), width)
        entries = wide[:, at]
        high = entries.astype(BF16)
        low = (entries - high.astype(F32)).astype(BF16)
        value = jnp.dot(side, jnp.concatenate([high, low], axis=0), preferred_element_type=F32)
        value_high = value.astype(BF16)
        image[0:LANES, at] = value_high
        image[LANES : 2 * LANES, at] = (value - value_high.astype(F32)).astype(BF16)
        return 0

    steps = columns // width
    cuts = [0] + [(steps * (k + 2)) // 5 for k in range(3)] + [steps]
    for k in range(4):
        lax.fori_loop(cuts[k], cuts[k + 1], image_step, 0)
        right.step(k + 1)
    right.step(5)
    right.step(6)
    left.step(0)
    right.step(7)
    right.step(8)
    left.step(1)
    left.step(2)
    right.step(9)

    image_acc[...] = jnp.zeros_like(image_acc)
    span = step_of(columns, 5120)

    def core_step(i, _):
        at = pl.ds(pl.multiple_of(i * span, span), span)
        factor = raw_right[:, :, :, :, at].reshape(LANES, span)
        image_acc[...] += lax.dot_general(
            image[:, at], factor, (((1,), (1,)), ((), ())), preferred_element_type=F32
        )
        return 0

    lax.fori_loop(0, columns // span, core_step, 0)
    core_part[...] = image_acc[0:LANES] + image_acc[LANES : 2 * LANES]

    part_rows = LANES // 2
    mine = pl.ds(pl.multiple_of(here.c * part_rows, part_rows), part_rows)
    theirs = pl.ds(pl.multiple_of((1 - here.c) * part_rows, part_rows), part_rows)
    core_swap = to_sibling(here, core_part.at[theirs], core_sib, sib_send, sib_recv, 0)
    core_swap.start()
    left.step(3)
    core_swap.wait_recv()
    core_x[here.x] = core_part[mine] + core_sib[...]
    sum_x = Exchange(here, core_x, small_send.at[0], small_recv.at[0], "x")
    sum_x.start()
    left.step(4)
    left.step(5)
    sum_x.wait()
    core_y[here.y] = added([core_x[k] for k in range(SIDE)])
    sum_y = Exchange(here, core_y, small_send.at[1], small_recv.at[1], "y")
    sum_y.start()
    left.step(6)
    left.step(7)
    sum_y.wait()
    core_z[here.z] = added([core_y[k] for k in range(SIDE)])
    sum_z = Exchange(here, core_z, small_send.at[2], small_recv.at[2], "z")
    sum_z.start()
    left.step(8)
    sum_z.wait()
    core_half[here.c] = added([core_z[k] for k in range(SIDE)]).astype(BF16)
    half_swap = to_sibling(here, core_half.at[here.c], core_half.at[here.c], sib_send, sib_recv, 1)
    half_swap.start()
    for k in range(4, 8):
        loads[k].wait()
    left.step(9)
    to_sibling(here, core_half.at[1 - here.c], core_half.at[1 - here.c], sib_send, sib_recv, 1).wait_recv()
    core = core_half[...].reshape(LANES, LANES)
    rows_cost = jnp.dot(src_left[...], core, preferred_element_type=F32).astype(BF16)

    peaks[...] = jnp.full_like(peaks, -jnp.inf)
    tiles = span // LANES

    def score_step(i, _):
        at = pl.ds(pl.multiple_of(i * span, span), span)
        factor = raw_left[:, :, :, :, at].reshape(LANES, span)
        score = jnp.dot(rows_cost, factor, preferred_element_type=F32) * SCORE
        wide[:, at] = score
        peak = peaks[...]
        for q in range(tiles):
            shift = tgt_potential[pl.ds(i * tiles + q, 1), :] * LOG2E
            peak = jnp.maximum(peak, score[:, q * LANES : (q + 1) * LANES] + shift)
        peaks[...] = peak
        return 0

    lax.fori_loop(0, columns // span, score_step, 0)

    totals[...] = jnp.zeros_like(totals)
    reach = step_of(columns, 3072)
    pieces = reach // LANES

    def total_step(i, _):
        peak = peaks[...]
        total = totals[...]
        for q in range(pieces):
            at = pl.ds(pl.multiple_of(i * reach + q * LANES, LANES), LANES)
            shift = tgt_potential[pl.ds(i * pieces + q, 1), :] * LOG2E
            total = total + jnp.exp2(wide[:, at] + shift - peak)
        totals[...] = total
        return 0

    lax.fori_loop(0, columns // reach, total_step, 0)
    lane_peak = peaks[...].T
    row_peak = jnp.max(lane_peak, axis=0, keepdims=True)
    row_total = jnp.sum(totals[...].T * jnp.exp2(lane_peak - row_peak), axis=0, keepdims=True)
    row_parts[here.x] = jnp.broadcast_to(row_peak + jnp.log2(row_total), row_parts.shape[1:])
    rows_x = Exchange(here, row_parts, small_send.at[3], small_recv.at[3], "x")
    rows_x.start()
    rows_x.wait()
    row_sum = merged([row_parts[k] for k in range(SIDE)])[0:1]
    row_potential = log_src[...] - LN2 * row_sum
    row_out[...] = row_potential
    row_shift_out[...] = jnp.broadcast_to(row_potential * LOG2E, (LANES, LANES)).T

    def col_step(i, _):
        for q in range(pieces):
            at = pl.ds(pl.multiple_of(i * reach + q * LANES, LANES), LANES)
            score = (wide[:, at] + row_shift_out[...]).reshape(rows // 8, 8, LANES)
            peak = jnp.max(score, axis=0)
            total = jnp.sum(jnp.exp2(score - peak[None]), axis=0)
            top = jnp.max(peak, axis=0, keepdims=True)
            total = jnp.sum(total * jnp.exp2(peak - top), axis=0, keepdims=True)
            col_all[pl.ds(i * pieces + q, 1), :] = top + jnp.log2(total)
        return 0

    lax.fori_loop(0, columns // reach, col_step, 0)

    col_rows = col_all.shape[0]
    some = col_sib.shape[0]
    rest = col_rows - some
    mine = pl.ds(pl.multiple_of(here.c * rest, 8), some)
    theirs = pl.ds(pl.multiple_of((1 - here.c) * rest, 8), some)
    col_swap = to_sibling(here, col_all.at[theirs], col_sib, sib_send, sib_recv, 2)
    col_swap.start()
    col_swap.wait_recv()
    col_z[here.z] = merged([col_all[mine, :], col_sib[...]])
    sum_z2 = Exchange(here, col_z, small_send.at[4], small_recv.at[4], "z")
    sum_z2.start()
    sum_z2.wait()
    col_y[here.y] = merged([col_z[k] for k in range(SIDE)])
    sum_y2 = Exchange(here, col_y, small_send.at[5], small_recv.at[5], "y")
    sum_y2.start()
    right.finish()
    left.finish()
    sum_y2.wait()
    col_out[mine, :] = log_tgt[mine, :] - LN2 * merged([col_y[k] for k in range(SIDE)])
    sent = pl.ds(pl.multiple_of(here.c * some, 8), rest)
    taken = pl.ds(pl.multiple_of((1 - here.c) * some, 8), rest)
    col_share = to_sibling(here, col_out.at[sent], col_out.at[sent], sib_send, sib_recv, 3)
    col_share.start()
    to_sibling(here, col_out.at[taken], col_out.at[taken], sib_send, sib_recv, 3).wait_recv()

    for exchange in (sum_x, sum_y, sum_z, rows_x, sum_z2, sum_y2):
        exchange.finish()
    for copy in (core_swap, half_swap, col_swap, col_share):
        copy.wait_send()


def plan_kernel(source_count, score, row_shift, row_in, col_in, plan, row_out, col_out):
    i = pl.program_id(0)
    row_out[...] = row_in[...]
    width = plan.shape[1]
    tiles = width // LANES
    for q in range(tiles):
        piece = pl.ds(i * tiles + q, 1)
        potential = col_in[piece, :]
        col_out[piece, :] = potential
        at = pl.ds(pl.multiple_of(i * width + q * LANES, LANES), LANES)
        shift = potential * LOG2E + math.log2(source_count)
        plan[:, q * LANES : (q + 1) * LANES] = jnp.exp2(score[:, at] + row_shift[...] + shift)


def per_device(
    coupling,
    src_left,
    emitter_distance_rightside,
    destination_distance_leftside,
    tgt_right,
    log_src,
    logarithm_destination_masses,
    tgt_potential,
):
    rows, columns = coupling.shape
    rank = src_left.shape[1]
    col_rows = columns // LANES
    some = -(-col_rows // 16) * 8
    source_count = rows * lax.axis_size("row")
    blocks = (SIDE, SIDE, 2, SHARE, columns)
    vmem = pl.BlockSpec(memory_space=pltpu.VMEM)
    anywhere = pl.BlockSpec(memory_space=pl.ANY)
    inputs = [
        coupling,
        tgt_right,
        destination_distance_leftside,
        src_left,
        emitter_distance_rightside,
        log_src.reshape(1, rows),
        logarithm_destination_masses.reshape(col_rows, LANES),
        tgt_potential.reshape(col_rows, LANES),
    ]
    outputs = pl.pallas_call(
        main_kernel,
        name="main",
        out_shape=[
            pltpu.VMEM((rows, columns), F32),
            pltpu.VMEM((rows, LANES), F32),
            pltpu.VMEM((1, rows), F32),
            pltpu.VMEM((col_rows, LANES), F32),
        ],
        in_specs=[anywhere] * len(inputs),
        out_specs=[vmem] * 4,
        scratch_shapes=[
            pltpu.VMEM(blocks, BF16),
            pltpu.VMEM(blocks, BF16),
            pltpu.VMEM((2 * rank, columns), BF16),
            pltpu.VMEM((rank, rank), F32),
            pltpu.VMEM((rank // 2, rank), F32),
            pltpu.VMEM((SIDE, rank // 2, rank), F32),
            pltpu.VMEM((SIDE, rank // 2, rank), F32),
            pltpu.VMEM((SIDE, rank // 2, rank), F32),
            pltpu.VMEM((2, rank // 2, rank), BF16),
            pltpu.VMEM((rows, LANES), F32),
            pltpu.VMEM((rows, LANES), F32),
            pltpu.VMEM((SIDE, 8, LANES), F32),
            pltpu.VMEM((col_rows, LANES), F32),
            pltpu.VMEM((some, LANES), F32),
            pltpu.VMEM((SIDE, some, LANES), F32),
            pltpu.VMEM((SIDE, some, LANES), F32),
            pltpu.VMEM((2 * rank, rank), F32),
            pltpu.VMEM((rows, rank), BF16),
            pltpu.VMEM((rows, rank), BF16),
            pltpu.VMEM((1, rows), F32),
            pltpu.VMEM((col_rows, LANES), F32),
            pltpu.VMEM((col_rows, LANES), F32),
            pltpu.SemaphoreType.DMA((len(inputs),)),
            pltpu.SemaphoreType.DMA((2 * Gather.MESSAGES,)),
            pltpu.SemaphoreType.DMA((2 * Gather.MESSAGES,)),
            pltpu.SemaphoreType.DMA((2 * Gather.MESSAGES,)),
            pltpu.SemaphoreType.DMA((2 * Gather.MESSAGES,)),
            pltpu.SemaphoreType.DMA((6, 3)),
            pltpu.SemaphoreType.DMA((6, 3)),
            pltpu.SemaphoreType.DMA((4,)),
            pltpu.SemaphoreType.DMA((4,)),
        ],
        compiler_params=pltpu.CompilerParams(
            collective_id=0, has_side_effects=True, vmem_limit_bytes=44 * 1024 * 1024
        ),
    )(*[pltpu.with_memory_space_constraint(array, pltpu.HBM) for array in inputs])
    outputs = [pltpu.with_memory_space_constraint(array, pltpu.VMEM) for array in outputs]
    width = step_of(columns, 3072)
    whole = lambda *shape: pl.BlockSpec(shape, lambda i: (0,) * len(shape))
    plan, row_potential, col_potential = pl.pallas_call(
        functools.partial(plan_kernel, source_count),
        name="plan",
        grid=(columns // width,),
        out_shape=[
            jax.ShapeDtypeStruct((rows, columns), F32),
            jax.ShapeDtypeStruct((1, rows), F32),
            jax.ShapeDtypeStruct((col_rows, LANES), F32),
        ],
        in_specs=[vmem] * 4,
        out_specs=[pl.BlockSpec((rows, width), lambda i: (0, i)), whole(1, rows), whole(col_rows, LANES)],
        compiler_params=pltpu.CompilerParams(vmem_limit_bytes=32 * 1024 * 1024),
    )(*outputs)
    return plan, row_potential.reshape(rows), col_potential.reshape(columns)


def solution(mesh):
    return jax.shard_map(
        per_device,
        mesh=mesh,
        in_specs=(
            P("row", "col"),
            P("row", None),
            P("row", None),
            P("row", "col"),
            P("row", "col"),
            P("row"),
            P("col"),
            P("col"),
        ),
        out_specs=(P("row", "col"), P("row"), P("col")),
        check_vma=False,
    )
```

time: 80.7 us -> 66.7 us (0.83)
  Pallas kernels: 74.5 us -> 65.9 us
  local copies, waits for them, and re-layouts: 5.16 us -> 0 us
    pallas_call x1, Pallas kernels: 68.3 us -> 61.7 us  [per_device(): pl.pallas_call(main_kernel, name='main', out_shape=[pltpu.VMEM((rows, col...]
    unnamed x10 -> x0, local copies, waits for them, and re-layouts: 5.16 us -> none
    pallas_call x1, Pallas kernels: 6.16 us -> 4.18 us  [per_device(): pl.pallas_call(functools.partial(plan_kernel, source_count), name='plan',...]
where the time goes in v2:
time: 66.7 us; the launch traced here: 66.6 us
  Pallas kernels  65.9 us (99%)
    pallas_call x1, Pallas kernels, per_device(): pl.pallas_call(main_kernel, name='main', out_shape=[pltpu.VMEM((rows, col...  61.7 us
    pallas_call x1, Pallas kernels, per_device(): pl.pallas_call(functools.partial(plan_kernel, source_count), name='plan',...  4.18 us

profile of v2, /device:TPU:1, one launch (start us, length us, event | category | flops | bytes accessed | tf_op | source)
XLA Modules:
  0.0 66.6 jit_solution(8038296040847074304)
XLA Ops:
  0.6 61.7 %main.1 = (f32[128,15360]{1,0:T(8,128)S(1)}, f32[128,128]{1,0:T(8,128)S(1)}, f32[1,128]{1,0:T(1,128)S(1)}, f32[120,128]{1,0:T(8,128)S(1)}) custom-call(f32[128,15360]{1,0:T(8,128)} %coupling_hbm.1, bf16[4,15360]{1,0:T(4,128)(2,1)} %tgt_right_hbm.1, bf16[4,15360]{1,0:T(4,128)(2,1)} %tgt_left_hbm.1, bf16[128,128]{1,0:T(8,128)(2,1)} %src_left_hbm.1, ...), custom_call_target="tpu_custom_call" | custom-call | tf_op jit(solution)/shard_map/main/pallas_call | solution.py:541
  62.4 4.2 %plan.1 = (f32[128,15360]{1,0:T(8,128)}, f32[1,128]{1,0:T(1,128)}, f32[120,128]{1,0:T(8,128)}) custom-call(f32[128,15360]{1,0:T(8,128)S(1)} %get-tuple-element.10.score, f32[128,128]{1,0:T(8,128)S(1)} %get-tuple-element.11.row_shift, f32[1,128]{1,0:T(1,128)S(1)} %get-tuple-element.12.row_in, f32[120,128]{1,0:T(8,128)S(1)} %get-tuple-element.13.col_in), custom_call_target="tpu_custom_call" | custom-call | tf_op jit(solution)/shard_map/plan/pallas_call | solution.py:592

commit v3 on v2

--- a/solution.py
+++ b/solution.py
@@ -31,22 +31,27 @@
         self.y = lax.div(row, 2 * SIDE)
         self.z = lax.rem(lax.div(row, 2), SIDE)
         self.c = lax.rem(row, 2)
+        self.near = {axis: {step: wrap(getattr(self, axis) + step) for step in (-1, 0, 1, 2)} for axis in "xyz"}
+        self.ids = {}
 
     def other(self, dx=0, dy=0, dz=0, dc=0):
-        core = 1 - self.c if dc else self.c
-        row = (wrap(self.y + dy) * SIDE + wrap(self.z + dz)) * 2 + core
-        return {"row": row, "col": wrap(self.x + dx)}
+        key = (dx, dy, dz, dc)
+        if key not in self.ids:
+            core = 1 - self.c if dc else self.c
+            row = (self.near["y"][dy] * SIDE + self.near["z"][dz]) * 2 + core
+            self.ids[key] = {"row": row, "col": self.near["x"][dx]}
+        return self.ids[key]
 
 
 class Gather:
     KINDS = ("A", "B")
-    MESSAGES = 37
+    RECEIVES = 41
+    SENDS = 3
 
     def __init__(self, here, raw, send, recv):
         self.here, self.raw, self.send, self.recv = here, raw, send, recv
         columns = raw.shape[-1]
         self.half, self.quarter = columns // 2, columns // 4
-        self.started = []
 
     def ref(self, kind, a, b, part, core=None):
         h = self.here
@@ -57,28 +62,26 @@
         else:
             columns = pl.ds(start + part * self.quarter, self.quarter)
         dy, dz = (a, b) if kind == "A" else (b, a)
-        y = slice(None) if dy is None else wrap(h.y + dy)
-        z = slice(None) if dz is None else wrap(h.z + dz)
+        y = slice(None) if dy is None else h.near["y"][dy]
+        z = slice(None) if dz is None else h.near["z"][dz]
         return self.raw.at[y, z, core, :, columns]
 
-    def copy(self, kind, number, ref, device):
-        index = number + (0 if kind == "A" else self.MESSAGES)
+
+    def copy(self, send, receive, ref, device):
         return pltpu.make_async_remote_copy(
             src_ref=ref,
             dst_ref=ref,
-            send_sem=self.send.at[index],
-            recv_sem=self.recv.at[index],
+            send_sem=self.send.at[send],
+            recv_sem=self.recv.at[receive],
             device_id=device,
             device_id_type=MESH,
         )
 
-    def start(self, kind, number, ref, device):
-        copy = self.copy(kind, number, ref, device)
-        copy.start()
-        self.started.append(copy)
-
-    def wait(self, kind, number, ref):
-        self.copy(kind, number, ref, self.here.other(dc=1)).wait_recv()
+    def start(self, send, receive, ref, device):
+        self.copy(send, receive, ref, device).start()
+
+    def wait(self, receive, ref):
+        self.copy(0, receive, ref, self.here.other(dc=1)).wait_recv()
 
     def along(self, kind, first, step):
         if first == (kind == "A"):
@@ -90,48 +93,52 @@
     def side(step):
         return 0 if step == 1 else 1
 
-    def first_number(self, part, step):
-        return part * 2 + self.side(step)
-
-    def last_number(self, b, part, step):
-        return 6 + (b + 1) * 4 + part * 2 + self.side(step)
-
-    def on_number(self, b, step):
-        return 22 + (b + 1) * 2 + self.side(step)
+    def number(self, kind, number):
+        return number + (0 if kind == "A" else 20)
+
+    def first_number(self, kind, part, step):
+        return self.number(kind, part * 2 + self.side(step))
+
+    def last_number(self, kind, b, part, step):
+        ends = part != self.side(step)
+        return self.number(kind, 14 + self.side(step) if ends else 8 + 2 * b + part)
 
     def first(self, kind, part, step):
-        self.start(kind, self.first_number(part, step), self.ref(kind, 0, 0, part), self.along(kind, True, step))
+        number = self.first_number(kind, part, step)
+        self.start(0, number, self.ref(kind, 0, 0, part), self.along(kind, True, step))
 
     def wait_first(self, kind, part, step):
-        self.wait(kind, self.first_number(part, step), self.ref(kind, 0, -step, part))
+        self.wait(self.first_number(kind, part, step), self.ref(kind, 0, -step, part))
 
     def first_on(self, kind, step):
         part = self.side(step)
-        self.start(kind, 4 + part, self.ref(kind, 0, -step, part), self.along(kind, True, step))
+        self.start(0, self.number(kind, 4 + part), self.ref(kind, 0, -step, part), self.along(kind, True, step))
 
     def wait_first_on(self, kind, step):
         part = self.side(step)
-        self.wait(kind, 4 + part, self.ref(kind, 0, 2, part))
+        self.wait(self.number(kind, 4 + part), self.ref(kind, 0, 2, part))
 
     def last(self, kind, b, part, step):
-        self.start(kind, self.last_number(b, part, step), self.ref(kind, 0, b, part), self.along(kind, False, step))
-
-    def wait_last(self, kind, b, part, step):
-        self.wait(kind, self.last_number(b, part, step), self.ref(kind, -step, b, part))
+        number = self.last_number(kind, b, part, step)
+        self.start(1, number, self.ref(kind, 0, b, part), self.along(kind, False, step))
+
+    def wait_last(self, kind, b, step):
+        part = self.side(step)
+        self.wait(self.last_number(kind, b, part, step), self.ref(kind, -step, b, part))
+
+    def wait_ending(self, kind, step):
+        part = 1 - self.side(step)
+        self.wait(self.last_number(kind, 0, part, step), self.ref(kind, -step, None, part))
 
     def last_on(self, kind, b, step):
         part = self.side(step)
-        self.start(kind, self.on_number(b, step), self.ref(kind, -step, b, part), self.along(kind, False, step))
-
-    def wait_last_on(self, kind, b, step):
-        part = self.side(step)
-        self.wait(kind, self.on_number(b, step), self.ref(kind, 2, b, part))
-
-    def to_sibling(self, kind, number, a, b):
-        self.start(kind, 30 + number, self.ref(kind, a, b, None), self.here.other(dc=1))
-
-    def wait_sibling(self, kind, number, a, b):
-        self.wait(kind, 30 + number, self.ref(kind, a, b, None, 1 - self.here.c))
+        self.start(1, self.number(kind, 17 + b), self.ref(kind, -step, b, part), self.along(kind, False, step))
+
+    def wait_last_on(self, kind, b):
+        self.wait(self.number(kind, 17 + b), self.ref(kind, 2, b, None))
+
+    def to_sibling(self, kind, a, b):
+        self.start(2, 40, self.ref(kind, a, b, None), self.here.other(dc=1))
 
     STEPS = ((1, 0), (-1, 1))
 
@@ -168,7 +175,7 @@
     def step_3(self):
         for kind in self.KINDS:
             for step, part in self.STEPS:
-                self.wait_last(kind, 0, part, step)
+                self.wait_last(kind, 0, step)
                 self.last_on(kind, 0, step)
         for kind in self.KINDS:
             for b in (-1, 1):
@@ -181,13 +188,13 @@
                 self.wait_first_on(kind, step)
                 self.last(kind, 2, part, step)
         for kind in self.KINDS:
-            self.to_sibling(kind, 0, 0, None)
+            self.to_sibling(kind, 0, None)
 
     def step_5(self):
         for kind in self.KINDS:
             for b in (-1, 1):
                 for step, part in self.STEPS:
-                    self.wait_last(kind, b, part, step)
+                    self.wait_last(kind, b, step)
                     self.last_on(kind, b, step)
         for kind in self.KINDS:
             for step, part in self.STEPS:
@@ -196,71 +203,54 @@
     def step_6(self):
         for kind in self.KINDS:
             for step, part in self.STEPS:
-                self.wait_last(kind, 2, part, step)
+                self.wait_last(kind, 2, step)
                 self.last_on(kind, 2, step)
 
     def step_7(self):
         for kind in self.KINDS:
-            for step, part in self.STEPS:
-                for b in (0, -1, 1, 2):
-                    self.wait_last(kind, b, 1 - part, step)
-                self.to_sibling(kind, 1 + part, -step, None)
+            for step, _ in self.STEPS:
+                self.wait_ending(kind, step)
+                self.to_sibling(kind, -step, None)
 
     def step_8(self):
-        for k, b in enumerate((0, -1, 1, 2)):
+        for b in (0, -1, 1, 2):
             for kind in self.KINDS:
-                for step, part in self.STEPS:
-                    self.wait_last_on(kind, b, step)
-                self.to_sibling(kind, 3 + k, 2, b)
+                self.wait_last_on(kind, b)
+                self.to_sibling(kind, 2, b)
 
     def step_9(self):
-        for kind in self.KINDS:
-            for k, a in enumerate((0, -1, 1)):
-                self.wait_sibling(kind, k, a, None)
-            for k, b in enumerate((0, -1, 1, 2)):
-                self.wait_sibling(kind, 3 + k, 2, b)
+        self.wait(40, self.raw.at[:, :, 1 - self.here.c])
 
     def finish(self):
-        for copy in self.started:
-            copy.wait_send()
+        for send, ref in enumerate((self.raw.at[0, 0:3, 0], self.raw.at[0:3, :, 0], self.raw.at[:, :, 0])):
+            self.copy(send, 0, ref, self.here.other(dc=1)).wait_send()
 
 
 class Exchange:
-    def __init__(self, here, buffer, send, recv, axis):
-        self.here, self.buffer, self.send, self.recv, self.axis = here, buffer, send, recv, axis
-        self.me = getattr(here, axis)
-
-    def copies(self):
-        for k, step in enumerate((1, -1, 2)):
-            ref = self.buffer.at[self.me]
-            yield pltpu.make_async_remote_copy(
-                src_ref=ref,
-                dst_ref=ref,
-                send_sem=self.send.at[k],
-                recv_sem=self.recv.at[k],
-                device_id=self.here.other(**{"d" + self.axis: step}),
-                device_id_type=MESH,
-            )
+    def __init__(self, here, buffer, send, recv, number, axis):
+        self.here, self.buffer, self.axis = here, buffer, axis
+        self.send, self.recv = send.at[number], recv.at[number]
+
+    def copy(self, ref, device):
+        return pltpu.make_async_remote_copy(
+            src_ref=ref,
+            dst_ref=ref,
+            send_sem=self.send,
+            recv_sem=self.recv,
+            device_id=device,
+            device_id_type=MESH,
+        )
 
     def start(self):
-        for copy in self.copies():
-            copy.start()
+        for step in (2, 1, -1):
+            own = self.buffer.at[getattr(self.here, self.axis)]
+            self.copy(own, self.here.other(**{"d" + self.axis: step})).start()
 
     def wait(self):
-        for k, step in enumerate((1, -1, 2)):
-            ref = self.buffer.at[wrap(self.me - step)]
-            pltpu.make_async_remote_copy(
-                src_ref=ref,
-                dst_ref=ref,
-                send_sem=self.send.at[k],
-                recv_sem=self.recv.at[k],
-                device_id=self.here.other(dc=1),
-                device_id_type=MESH,
-            ).wait_recv()
+        self.copy(self.buffer.at[0:3], self.here.other(dc=1)).wait_recv()
 
     def finish(self):
-        for copy in self.copies():
-            copy.wait_send()
+        self.copy(self.buffer.at[0:3], self.here.other(dc=1)).wait_send()
 
 
 def to_sibling(here, src, dst, send, recv, index):
@@ -382,19 +372,19 @@
     left.step(3)
     core_swap.wait_recv()
     core_x[here.x] = core_part[mine] + core_sib[...]
-    sum_x = Exchange(here, core_x, small_send.at[0], small_recv.at[0], "x")
+    sum_x = Exchange(here, core_x, small_send, small_recv, 0, "x")
     sum_x.start()
     left.step(4)
     left.step(5)
     sum_x.wait()
     core_y[here.y] = added([core_x[k] for k in range(SIDE)])
-    sum_y = Exchange(here, core_y, small_send.at[1], small_recv.at[1], "y")
+    sum_y = Exchange(here, core_y, small_send, small_recv, 1, "y")
     sum_y.start()
     left.step(6)
     left.step(7)
     sum_y.wait()
     core_z[here.z] = added([core_y[k] for k in range(SIDE)])
-    sum_z = Exchange(here, core_z, small_send.at[2], small_recv.at[2], "z")
+    sum_z = Exchange(here, core_z, small_send, small_recv, 2, "z")
     sum_z.start()
     left.step(8)
     sum_z.wait()
@@ -444,7 +434,7 @@
     row_peak = jnp.max(lane_peak, axis=0, keepdims=True)
     row_total = jnp.sum(totals[...].T * jnp.exp2(lane_peak - row_peak), axis=0, keepdims=True)
     row_parts[here.x] = jnp.broadcast_to(row_peak + jnp.log2(row_total), row_parts.shape[1:])
-    rows_x = Exchange(here, row_parts, small_send.at[3], small_recv.at[3], "x")
+    rows_x = Exchange(here, row_parts, small_send, small_recv, 3, "x")
     rows_x.start()
     rows_x.wait()
     row_sum = merged([row_parts[k] for k in range(SIDE)])[0:1]
@@ -474,11 +464,11 @@
     col_swap.start()
     col_swap.wait_recv()
     col_z[here.z] = merged([col_all[mine, :], col_sib[...]])
-    sum_z2 = Exchange(here, col_z, small_send.at[4], small_recv.at[4], "z")
+    sum_z2 = Exchange(here, col_z, small_send, small_recv, 4, "z")
     sum_z2.start()
     sum_z2.wait()
     col_y[here.y] = merged([col_z[k] for k in range(SIDE)])
-    sum_y2 = Exchange(here, col_y, small_send.at[5], small_recv.at[5], "y")
+    sum_y2 = Exchange(here, col_y, small_send, small_recv, 5, "y")
     sum_y2.start()
     right.finish()
     left.finish()
@@ -496,18 +486,25 @@
         copy.wait_send()
 
 
-def plan_kernel(source_count, score, row_shift, row_in, col_in, plan, row_out, col_out):
-    i = pl.program_id(0)
-    row_out[...] = row_in[...]
-    width = plan.shape[1]
-    tiles = width // LANES
-    for q in range(tiles):
-        piece = pl.ds(i * tiles + q, 1)
-        potential = col_in[piece, :]
-        col_out[piece, :] = potential
-        at = pl.ds(pl.multiple_of(i * width + q * LANES, LANES), LANES)
-        shift = potential * LOG2E + math.log2(source_count)
-        plan[:, q * LANES : (q + 1) * LANES] = jnp.exp2(score[:, at] + row_shift[...] + shift)
+def plan_kernel(source_count, score, row_shift, row_in, col_in, plan, row_out, col_out, buffer, done):
+    pieces = done.shape[0] - 2
+    width = buffer.shape[1] // pieces
+    copies = [
+        pltpu.make_async_copy(row_in, row_out, done.at[pieces]),
+        pltpu.make_async_copy(col_in, col_out, done.at[pieces + 1]),
+    ]
+    for copy in copies:
+        copy.start()
+    for i in range(pieces):
+        for q in range(i * width // LANES, (i + 1) * width // LANES):
+            at = pl.ds(q * LANES, LANES)
+            shift = col_in[pl.ds(q, 1), :] * LOG2E + math.log2(source_count)
+            buffer[:, at] = jnp.exp2(score[:, at] + row_shift[...] + shift)
+        at = pl.ds(i * width, width)
+        copies.append(pltpu.make_async_copy(buffer.at[:, at], plan.at[:, at], done.at[i]))
+        copies[-1].start()
+    for copy in copies:
+        copy.wait()
 
 
 def per_device(
@@ -573,12 +570,12 @@
             pltpu.VMEM((col_rows, LANES), F32),
             pltpu.VMEM((col_rows, LANES), F32),
             pltpu.SemaphoreType.DMA((len(inputs),)),
-            pltpu.SemaphoreType.DMA((2 * Gather.MESSAGES,)),
-            pltpu.SemaphoreType.DMA((2 * Gather.MESSAGES,)),
-            pltpu.SemaphoreType.DMA((2 * Gather.MESSAGES,)),
-            pltpu.SemaphoreType.DMA((2 * Gather.MESSAGES,)),
-            pltpu.SemaphoreType.DMA((6, 3)),
-            pltpu.SemaphoreType.DMA((6, 3)),
+            pltpu.SemaphoreType.DMA((Gather.SENDS,)),
+            pltpu.SemaphoreType.DMA((Gather.RECEIVES,)),
+            pltpu.SemaphoreType.DMA((Gather.SENDS,)),
+            pltpu.SemaphoreType.DMA((Gather.RECEIVES,)),
+            pltpu.SemaphoreType.DMA((6,)),
+            pltpu.SemaphoreType.DMA((6,)),
             pltpu.SemaphoreType.DMA((4,)),
             pltpu.SemaphoreType.DMA((4,)),
         ],
@@ -587,19 +584,18 @@
         ),
     )(*[pltpu.with_memory_space_constraint(array, pltpu.HBM) for array in inputs])
     outputs = [pltpu.with_memory_space_constraint(array, pltpu.VMEM) for array in outputs]
-    width = step_of(columns, 3072)
-    whole = lambda *shape: pl.BlockSpec(shape, lambda i: (0,) * len(shape))
+    pieces = columns // step_of(columns, 768)
     plan, row_potential, col_potential = pl.pallas_call(
         functools.partial(plan_kernel, source_count),
         name="plan",
-        grid=(columns // width,),
         out_shape=[
             jax.ShapeDtypeStruct((rows, columns), F32),
             jax.ShapeDtypeStruct((1, rows), F32),
             jax.ShapeDtypeStruct((col_rows, LANES), F32),
         ],
         in_specs=[vmem] * 4,
-        out_specs=[pl.BlockSpec((rows, width), lambda i: (0, i)), whole(1, rows), whole(col_rows, LANES)],
+        out_specs=[anywhere] * 3,
+        scratch_shapes=[pltpu.VMEM((rows, columns), F32), pltpu.SemaphoreType.DMA((pieces + 2,))],
         compiler_params=pltpu.CompilerParams(vmem_limit_bytes=32 * 1024 * 1024),
     )(*outputs)
     return plan, row_potential.reshape(rows), col_potential.reshape(columns)

time: 66.7 us -> 62.8 us (0.942)
  Pallas kernels: 65.9 us -> 62.1 us
    pallas_call x1, Pallas kernels: 61.7 us -> 58.7 us  [per_device(): pl.pallas_call(main_kernel, name='main', out_shape=[pltpu.VMEM((rows, col...]
    pallas_call x1, Pallas kernels: 4.18 us -> 3.37 us  [per_device(): pl.pallas_call(functools.partial(plan_kernel, source_count), name='plan',...]
where the time goes in v3:
time: 62.8 us; the launch traced here: 62.7 us
  Pallas kernels  62.1 us (99%)
  between operations  0.64 us (1%)
    pallas_call x1, Pallas kernels, per_device(): pl.pallas_call(main_kernel, name='main', out_shape=[pltpu.VMEM((rows, col...  58.7 us
    pallas_call x1, Pallas kernels, per_device(): pl.pallas_call(functools.partial(plan_kernel, source_count), name='plan',...  3.37 us

profile of v3, /device:TPU:1, one launch (start us, length us, event | category | flops | bytes accessed | tf_op | source)
XLA Modules:
  0.0 62.7 jit_solution(4760473948827336)
XLA Ops:
  0.6 58.7 %main.1 = (f32[128,15360]{1,0:T(8,128)S(1)}, f32[128,128]{1,0:T(8,128)S(1)}, f32[1,128]{1,0:T(1,128)S(1)}, f32[120,128]{1,0:T(8,128)S(1)}) custom-call(f32[128,15360]{1,0:T(8,128)} %coupling_hbm.1, bf16[4,15360]{1,0:T(4,128)(2,1)} %tgt_right_hbm.1, bf16[4,15360]{1,0:T(4,128)(2,1)} %tgt_left_hbm.1, bf16[128,128]{1,0:T(8,128)(2,1)} %src_left_hbm.1, ...), custom_call_target="tpu_custom_call" | custom-call | tf_op jit(solution)/shard_map/main/pallas_call | solution.py:538
  59.4 3.4 %plan.1 = (f32[128,15360]{1,0:T(8,128)}, f32[1,128]{1,0:T(1,128)}, f32[120,128]{1,0:T(8,128)}) custom-call(f32[128,15360]{1,0:T(8,128)S(1)} %get-tuple-element.10.score, f32[128,128]{1,0:T(8,128)S(1)} %get-tuple-element.11.row_shift, f32[1,128]{1,0:T(1,128)S(1)} %get-tuple-element.12.row_in, f32[120,128]{1,0:T(8,128)S(1)} %get-tuple-element.13.col_in), custom_call_target="tpu_custom_call" | custom-call | tf_op jit(solution)/shard_map/plan/pallas_call | solution.py:588

commit v4 on v3

--- a/solution.py
+++ b/solution.py
@@ -137,8 +137,8 @@
     def wait_last_on(self, kind, b):
         self.wait(self.number(kind, 17 + b), self.ref(kind, 2, b, None))
 
-    def to_sibling(self, kind, a, b):
-        self.start(2, 40, self.ref(kind, a, b, None), self.here.other(dc=1))
+    def to_sibling(self, kind, a, b, part=None):
+        self.start(2, 40, self.ref(kind, a, b, part), self.here.other(dc=1))
 
     STEPS = ((1, 0), (-1, 1))
 
@@ -205,12 +205,15 @@
             for step, part in self.STEPS:
                 self.wait_last(kind, 2, step)
                 self.last_on(kind, 2, step)
+        for kind in self.KINDS:
+            for step, part in self.STEPS:
+                self.to_sibling(kind, -step, None, part)
 
     def step_7(self):
         for kind in self.KINDS:
-            for step, _ in self.STEPS:
+            for step, part in self.STEPS:
                 self.wait_ending(kind, step)
-                self.to_sibling(kind, -step, None)
+                self.to_sibling(kind, -step, None, 1 - part)
 
     def step_8(self):
         for b in (0, -1, 1, 2):
@@ -282,8 +285,8 @@
     coupling_hbm, tgt_right_hbm, tgt_left_hbm,
     src_left_hbm, src_right_hbm, log_src_hbm, log_tgt_hbm, tgt_potential_hbm,
     wide, row_shift_out, row_out, col_out,
-    raw_right, raw_left, image, core_part, core_sib, core_x, core_y, core_z, core_half,
-    peaks, totals, row_parts, col_all, col_sib, col_z, col_y, image_acc,
+    raw_right, raw_left, image, core_part, core_sib, core_sums, core_half,
+    peaks, totals, row_parts, col_all, col_sib, col_sums,
     src_left, src_right, log_src, log_tgt, tgt_potential,
     local, right_send, right_recv, left_send, left_recv,
     small_send, small_recv, sib_send, sib_recv,
@@ -342,27 +345,17 @@
         lax.fori_loop(cuts[k], cuts[k + 1], image_step, 0)
         right.step(k + 1)
     right.step(5)
+    left.step(0)
     right.step(6)
-    left.step(0)
     right.step(7)
     right.step(8)
     left.step(1)
     left.step(2)
     right.step(9)
 
-    image_acc[...] = jnp.zeros_like(image_acc)
-    span = step_of(columns, 5120)
-
-    def core_step(i, _):
-        at = pl.ds(pl.multiple_of(i * span, span), span)
-        factor = raw_right[:, :, :, :, at].reshape(LANES, span)
-        image_acc[...] += lax.dot_general(
-            image[:, at], factor, (((1,), (1,)), ((), ())), preferred_element_type=F32
-        )
-        return 0
-
-    lax.fori_loop(0, columns // span, core_step, 0)
-    core_part[...] = image_acc[0:LANES] + image_acc[LANES : 2 * LANES]
+    factor = raw_right[...].reshape(LANES, columns)
+    parts = lax.dot_general(image[...], factor, (((1,), (1,)), ((), ())), preferred_element_type=F32)
+    core_part[...] = parts[0:LANES] + parts[LANES : 2 * LANES]
 
     part_rows = LANES // 2
     mine = pl.ds(pl.multiple_of(here.c * part_rows, part_rows), part_rows)
@@ -371,24 +364,36 @@
     core_swap.start()
     left.step(3)
     core_swap.wait_recv()
-    core_x[here.x] = core_part[mine] + core_sib[...]
-    sum_x = Exchange(here, core_x, small_send, small_recv, 0, "x")
-    sum_x.start()
+    total = core_part[mine] + core_sib[...]
+    piece = part_rows // 2
+    totals_of = [total[0:piece], total[piece:]]
+    sums = []
+
+    def sum_start(stage):
+        for p, order in enumerate(("xyz", "yzx")):
+            number = 2 * stage + p
+            core_sums[number, getattr(here, order[stage])] = totals_of[p]
+            sums.append(Exchange(here, core_sums.at[number], small_send, small_recv, number, order[stage]))
+            sums[-1].start()
+
+    def sum_wait(stage):
+        for p in range(2):
+            number = 2 * stage + p
+            sums[number].wait()
+            totals_of[p] = added([core_sums[number, k] for k in range(SIDE)])
+
+    sum_start(0)
     left.step(4)
     left.step(5)
-    sum_x.wait()
-    core_y[here.y] = added([core_x[k] for k in range(SIDE)])
-    sum_y = Exchange(here, core_y, small_send, small_recv, 1, "y")
-    sum_y.start()
+    sum_wait(0)
+    sum_start(1)
     left.step(6)
     left.step(7)
-    sum_y.wait()
-    core_z[here.z] = added([core_y[k] for k in range(SIDE)])
-    sum_z = Exchange(here, core_z, small_send, small_recv, 2, "z")
-    sum_z.start()
+    sum_wait(1)
+    sum_start(2)
     left.step(8)
-    sum_z.wait()
-    core_half[here.c] = added([core_z[k] for k in range(SIDE)]).astype(BF16)
+    sum_wait(2)
+    core_half[here.c] = jnp.concatenate(totals_of, axis=0).astype(BF16)
     half_swap = to_sibling(here, core_half.at[here.c], core_half.at[here.c], sib_send, sib_recv, 1)
     half_swap.start()
     for k in range(4, 8):
@@ -397,6 +402,8 @@
     to_sibling(here, core_half.at[1 - here.c], core_half.at[1 - here.c], sib_send, sib_recv, 1).wait_recv()
     core = core_half[...].reshape(LANES, LANES)
     rows_cost = jnp.dot(src_left[...], core, preferred_element_type=F32).astype(BF16)
+
+    span = step_of(columns, 5120)
 
     peaks[...] = jnp.full_like(peaks, -jnp.inf)
     tiles = span // LANES
@@ -434,7 +441,8 @@
     row_peak = jnp.max(lane_peak, axis=0, keepdims=True)
     row_total = jnp.sum(totals[...].T * jnp.exp2(lane_peak - row_peak), axis=0, keepdims=True)
     row_parts[here.x] = jnp.broadcast_to(row_peak + jnp.log2(row_total), row_parts.shape[1:])
-    rows_x = Exchange(here, row_parts, small_send, small_recv, 3, "x")
+    rows_x = Exchange(here, row_parts, small_send, small_recv, 6, "x")
+    sums.append(rows_x)
     rows_x.start()
     rows_x.wait()
     row_sum = merged([row_parts[k] for k in range(SIDE)])[0:1]
@@ -463,24 +471,37 @@
     col_swap = to_sibling(here, col_all.at[theirs], col_sib, sib_send, sib_recv, 2)
     col_swap.start()
     col_swap.wait_recv()
-    col_z[here.z] = merged([col_all[mine, :], col_sib[...]])
-    sum_z2 = Exchange(here, col_z, small_send, small_recv, 4, "z")
-    sum_z2.start()
-    sum_z2.wait()
-    col_y[here.y] = merged([col_z[k] for k in range(SIDE)])
-    sum_y2 = Exchange(here, col_y, small_send, small_recv, 5, "y")
-    sum_y2.start()
+    total = merged([col_all[mine, :], col_sib[...]])
+    piece = some // 2
+    totals_of[:] = [total[0:piece], total[piece:]]
+
+    def col_start(stage):
+        for p, order in enumerate(("zy", "yz")):
+            number = 2 * stage + p
+            col_sums[number, getattr(here, order[stage])] = totals_of[p]
+            sums.append(Exchange(here, col_sums.at[number], small_send, small_recv, 7 + number, order[stage]))
+            sums[-1].start()
+
+    def col_wait(stage):
+        for p in range(2):
+            number = 2 * stage + p
+            sums[7 + number].wait()
+            totals_of[p] = merged([col_sums[number, k] for k in range(SIDE)])
+
+    col_start(0)
+    col_wait(0)
+    col_start(1)
     right.finish()
     left.finish()
-    sum_y2.wait()
-    col_out[mine, :] = log_tgt[mine, :] - LN2 * merged([col_y[k] for k in range(SIDE)])
+    col_wait(1)
+    col_out[mine, :] = log_tgt[mine, :] - LN2 * jnp.concatenate(totals_of, axis=0)
     sent = pl.ds(pl.multiple_of(here.c * some, 8), rest)
     taken = pl.ds(pl.multiple_of((1 - here.c) * some, 8), rest)
     col_share = to_sibling(here, col_out.at[sent], col_out.at[sent], sib_send, sib_recv, 3)
     col_share.start()
     to_sibling(here, col_out.at[taken], col_out.at[taken], sib_send, sib_recv, 3).wait_recv()
 
-    for exchange in (sum_x, sum_y, sum_z, rows_x, sum_z2, sum_y2):
+    for exchange in sums:
         exchange.finish()
     for copy in (core_swap, half_swap, col_swap, col_share):
         copy.wait_send()
@@ -520,7 +541,7 @@
     rows, columns = coupling.shape
     rank = src_left.shape[1]
     col_rows = columns // LANES
-    some = -(-col_rows // 16) * 8
+    some = -(-col_rows // 32) * 16
     source_count = rows * lax.axis_size("row")
     blocks = (SIDE, SIDE, 2, SHARE, columns)
     vmem = pl.BlockSpec(memory_space=pltpu.VMEM)
@@ -552,18 +573,14 @@
             pltpu.VMEM((2 * rank, columns), BF16),
             pltpu.VMEM((rank, rank), F32),
             pltpu.VMEM((rank // 2, rank), F32),
-            pltpu.VMEM((SIDE, rank // 2, rank), F32),
-            pltpu.VMEM((SIDE, rank // 2, rank), F32),
-            pltpu.VMEM((SIDE, rank // 2, rank), F32),
+            pltpu.VMEM((6, SIDE, rank // 4, rank), F32),
             pltpu.VMEM((2, rank // 2, rank), BF16),
             pltpu.VMEM((rows, LANES), F32),
             pltpu.VMEM((rows, LANES), F32),
             pltpu.VMEM((SIDE, 8, LANES), F32),
             pltpu.VMEM((col_rows, LANES), F32),
             pltpu.VMEM((some, LANES), F32),
-            pltpu.VMEM((SIDE, some, LANES), F32),
-            pltpu.VMEM((SIDE, some, LANES), F32),
-            pltpu.VMEM((2 * rank, rank), F32),
+            pltpu.VMEM((4, SIDE, some // 2, LANES), F32),
             pltpu.VMEM((rows, rank), BF16),
             pltpu.VMEM((rows, rank), BF16),
             pltpu.VMEM((1, rows), F32),
@@ -574,8 +591,8 @@
             pltpu.SemaphoreType.DMA((Gather.RECEIVES,)),
             pltpu.SemaphoreType.DMA((Gather.SENDS,)),
             pltpu.SemaphoreType.DMA((Gather.RECEIVES,)),
-            pltpu.SemaphoreType.DMA((6,)),
-            pltpu.SemaphoreType.DMA((6,)),
+            pltpu.SemaphoreType.DMA((11,)),
+            pltpu.SemaphoreType.DMA((11,)),
             pltpu.SemaphoreType.DMA((4,)),
             pltpu.SemaphoreType.DMA((4,)),
         ],

time: 62.8 us -> 61 us (0.971)
  Pallas kernels: 62.1 us -> 60.2 us
    pallas_call x1, Pallas kernels: 58.7 us -> 56.9 us  [per_device(): pl.pallas_call(main_kernel, name='main', out_shape=[pltpu.VMEM((rows, col...]
where the time goes in v4:
time: 61 us; the launch traced here: 60.9 us
  Pallas kernels  60.2 us (99%)
  between operations  0.64 us (1%)
    pallas_call x1, Pallas kernels, per_device(): pl.pallas_call(main_kernel, name='main', out_shape=[pltpu.VMEM((rows, col...  56.9 us
    pallas_call x1, Pallas kernels, per_device(): pl.pallas_call(functools.partial(plan_kernel, source_count), name='plan',...  3.37 us

profile of v4, /device:TPU:1, one launch (start us, length us, event | category | flops | bytes accessed | tf_op | source)
XLA Modules:
  0.0 60.9 jit_solution(9568978968800174220)
XLA Ops:
  0.6 56.9 %main.1 = (f32[128,15360]{1,0:T(8,128)S(1)}, f32[128,128]{1,0:T(8,128)S(1)}, f32[1,128]{1,0:T(1,128)S(1)}, f32[120,128]{1,0:T(8,128)S(1)}) custom-call(f32[128,15360]{1,0:T(8,128)} %coupling_hbm.1, bf16[4,15360]{1,0:T(4,128)(2,1)} %tgt_right_hbm.1, bf16[4,15360]{1,0:T(4,128)(2,1)} %tgt_left_hbm.1, bf16[128,128]{1,0:T(8,128)(2,1)} %src_left_hbm.1, ...), custom_call_target="tpu_custom_call" | custom-call | tf_op jit(solution)/shard_map/main/pallas_call | solution.py:559
  57.5 3.4 %plan.1 = (f32[128,15360]{1,0:T(8,128)}, f32[1,128]{1,0:T(1,128)}, f32[120,128]{1,0:T(8,128)}) custom-call(f32[128,15360]{1,0:T(8,128)S(1)} %get-tuple-element.10.score, f32[128,128]{1,0:T(8,128)S(1)} %get-tuple-element.11.row_shift, f32[1,128]{1,0:T(1,128)S(1)} %get-tuple-element.12.row_in, f32[120,128]{1,0:T(8,128)S(1)} %get-tuple-element.13.col_in), custom_call_target="tpu_custom_call" | custom-call | tf_op jit(solution)/shard_map/plan/pallas_call | solution.py:605

commit v5 on v4

--- a/solution.py
+++ b/solution.py
@@ -295,6 +295,12 @@
     columns = wide.shape[1]
     rows = wide.shape[0]
 
+    barrier = pltpu.get_barrier_semaphore()
+    partners = [here.other(dc=1)]
+    for axis in "xyz":
+        partners += [here.other(**{"d" + axis: step}) for step in (1, -1, 2)]
+    for partner in partners:
+        pl.semaphore_signal(barrier, inc=1, device_id=partner, device_id_type=MESH)
     loads = []
     for k, (source, target) in enumerate((
         (tgt_right_hbm, raw_right.at[here.y, here.z, here.c]),
@@ -309,12 +315,6 @@
         loads.append(pltpu.make_async_copy(source, target, local.at[k]))
         loads[-1].start()
 
-    barrier = pltpu.get_barrier_semaphore()
-    partners = [here.other(dc=1)]
-    for axis in "xyz":
-        partners += [here.other(**{"d" + axis: step}) for step in (1, -1, 2)]
-    for partner in partners:
-        pl.semaphore_signal(barrier, inc=1, device_id=partner, device_id_type=MESH)
     loads[0].wait()
     pl.semaphore_wait(barrier, len(partners))
 
@@ -324,8 +324,7 @@
 
     for k in (1, 2, 3):
         loads[k].wait()
-    side = src_right[...].astype(F32).T.astype(BF16)
-    side = jnp.concatenate([side, side], axis=1)
+    side = jnp.concatenate([src_right[...], src_right[...]], axis=0)
     width = step_of(columns, 3072)
 
     def image_step(i, _):
@@ -333,14 +332,16 @@
         entries = wide[:, at]
         high = entries.astype(BF16)
         low = (entries - high.astype(F32)).astype(BF16)
-        value = jnp.dot(side, jnp.concatenate([high, low], axis=0), preferred_element_type=F32)
+        value = lax.dot_general(
+            jnp.concatenate([high, low], axis=0), side, (((0,), (0,)), ((), ())), preferred_element_type=F32
+        )
         value_high = value.astype(BF16)
-        image[0:LANES, at] = value_high
-        image[LANES : 2 * LANES, at] = (value - value_high.astype(F32)).astype(BF16)
+        image[at, 0:LANES] = value_high
+        image[at, LANES : 2 * LANES] = (value - value_high.astype(F32)).astype(BF16)
         return 0
 
     steps = columns // width
-    cuts = [0] + [(steps * (k + 2)) // 5 for k in range(3)] + [steps]
+    cuts = [0, 0, (steps * 2) // 5, (steps * 3) // 5, steps]
     for k in range(4):
         lax.fori_loop(cuts[k], cuts[k + 1], image_step, 0)
         right.step(k + 1)
@@ -354,8 +355,8 @@
     right.step(9)
 
     factor = raw_right[...].reshape(LANES, columns)
-    parts = lax.dot_general(image[...], factor, (((1,), (1,)), ((), ())), preferred_element_type=F32)
-    core_part[...] = parts[0:LANES] + parts[LANES : 2 * LANES]
+    parts = jnp.dot(factor, image[...], preferred_element_type=F32)
+    core_part[...] = parts[:, 0:LANES] + parts[:, LANES : 2 * LANES]
 
     part_rows = LANES // 2
     mine = pl.ds(pl.multiple_of(here.c * part_rows, part_rows), part_rows)
@@ -401,7 +402,9 @@
     left.step(9)
     to_sibling(here, core_half.at[1 - here.c], core_half.at[1 - here.c], sib_send, sib_recv, 1).wait_recv()
     core = core_half[...].reshape(LANES, LANES)
-    rows_cost = jnp.dot(src_left[...], core, preferred_element_type=F32).astype(BF16)
+    rows_cost = lax.dot_general(
+        src_left[...], core, (((1,), (1,)), ((), ())), preferred_element_type=F32
+    ).astype(BF16)
 
     span = step_of(columns, 5120)
 
@@ -570,7 +573,7 @@
         scratch_shapes=[
             pltpu.VMEM(blocks, BF16),
             pltpu.VMEM(blocks, BF16),
-            pltpu.VMEM((2 * rank, columns), BF16),
+            pltpu.VMEM((columns, 2 * rank), BF16),
             pltpu.VMEM((rank, rank), F32),
             pltpu.VMEM((rank // 2, rank), F32),
             pltpu.VMEM((6, SIDE, rank // 4, rank), F32),

time: 61 us -> 60.6 us (level)
  no operation moved by 1% of the time
where the time goes in v5:
time: 60.6 us; the launch traced here: 60.4 us
  Pallas kernels  59.8 us (99%)
  between operations  0.64 us (1%)
    pallas_call x1, Pallas kernels, per_device(): pl.pallas_call(main_kernel, name='main', out_shape=[pltpu.VMEM((rows, col...  56.4 us
    pallas_call x1, Pallas kernels, per_device(): pl.pallas_call(functools.partial(plan_kernel, source_count), name='plan',...  3.37 us

profile of v5, /device:TPU:1, one launch (start us, length us, event | category | flops | bytes accessed | tf_op | source)
XLA Modules:
  0.0 60.4 jit_solution(13973173591838821397)
XLA Ops:
  0.6 56.4 %main.1 = (f32[128,15360]{1,0:T(8,128)S(1)}, f32[128,128]{1,0:T(8,128)S(1)}, f32[1,128]{1,0:T(1,128)S(1)}, f32[120,128]{1,0:T(8,128)S(1)}) custom-call(f32[128,15360]{1,0:T(8,128)} %coupling_hbm.1, bf16[4,15360]{1,0:T(4,128)(2,1)} %tgt_right_hbm.1, bf16[4,15360]{1,0:T(4,128)(2,1)} %tgt_left_hbm.1, bf16[128,128]{1,0:T(8,128)(2,1)} %src_left_hbm.1, ...), custom_call_target="tpu_custom_call" | custom-call | tf_op jit(solution)/shard_map/main/pallas_call | solution.py:562
  57.1 3.4 %plan.1 = (f32[128,15360]{1,0:T(8,128)}, f32[1,128]{1,0:T(1,128)}, f32[120,128]{1,0:T(8,128)}) custom-call(f32[128,15360]{1,0:T(8,128)S(1)} %get-tuple-element.10.score, f32[128,128]{1,0:T(8,128)S(1)} %get-tuple-element.11.row_shift, f32[1,128]{1,0:T(1,128)S(1)} %get-tuple-element.12.row_in, f32[120,128]{1,0:T(8,128)S(1)} %get-tuple-element.13.col_in), custom_call_target="tpu_custom_call" | custom-call | tf_op jit(solution)/shard_map/plan/pallas_call | solution.py:608

commit v6 on v5

--- a/solution.py
+++ b/solution.py
@@ -230,9 +230,9 @@
 
 
 class Exchange:
-    def __init__(self, here, buffer, send, recv, number, axis):
+    def __init__(self, here, buffer, send, recv, axis):
         self.here, self.buffer, self.axis = here, buffer, axis
-        self.send, self.recv = send.at[number], recv.at[number]
+        self.send, self.recv = send, recv
 
     def copy(self, ref, device):
         return pltpu.make_async_remote_copy(
@@ -249,11 +249,12 @@
             own = self.buffer.at[getattr(self.here, self.axis)]
             self.copy(own, self.here.other(**{"d" + self.axis: step})).start()
 
-    def wait(self):
-        self.copy(self.buffer.at[0:3], self.here.other(dc=1)).wait_recv()
-
-    def finish(self):
-        self.copy(self.buffer.at[0:3], self.here.other(dc=1)).wait_send()
+    def wait(self, three_parts=None):
+        three_parts = self.buffer.at[0:3] if three_parts is None else three_parts
+        self.copy(three_parts, self.here.other(dc=1)).wait_recv()
+
+    def finish(self, three_parts):
+        self.copy(three_parts, self.here.other(dc=1)).wait_send()
 
 
 def to_sibling(here, src, dst, send, recv, index):
@@ -374,13 +375,13 @@
         for p, order in enumerate(("xyz", "yzx")):
             number = 2 * stage + p
             core_sums[number, getattr(here, order[stage])] = totals_of[p]
-            sums.append(Exchange(here, core_sums.at[number], small_send, small_recv, number, order[stage]))
+            sums.append(Exchange(here, core_sums.at[number], small_send.at[0], small_recv.at[stage], order[stage]))
             sums[-1].start()
 
     def sum_wait(stage):
+        sums[2 * stage].wait(core_sums.at[2 * stage : 2 * stage + 2, 0:3])
         for p in range(2):
             number = 2 * stage + p
-            sums[number].wait()
             totals_of[p] = added([core_sums[number, k] for k in range(SIDE)])
 
     sum_start(0)
@@ -406,7 +407,7 @@
         src_left[...], core, (((1,), (1,)), ((), ())), preferred_element_type=F32
     ).astype(BF16)
 
-    span = step_of(columns, 5120)
+    span = step_of(columns, 7680)
 
     peaks[...] = jnp.full_like(peaks, -jnp.inf)
     tiles = span // LANES
@@ -444,7 +445,7 @@
     row_peak = jnp.max(lane_peak, axis=0, keepdims=True)
     row_total = jnp.sum(totals[...].T * jnp.exp2(lane_peak - row_peak), axis=0, keepdims=True)
     row_parts[here.x] = jnp.broadcast_to(row_peak + jnp.log2(row_total), row_parts.shape[1:])
-    rows_x = Exchange(here, row_parts, small_send, small_recv, 6, "x")
+    rows_x = Exchange(here, row_parts, small_send.at[1], small_recv.at[3], "x")
     sums.append(rows_x)
     rows_x.start()
     rows_x.wait()
@@ -482,13 +483,13 @@
         for p, order in enumerate(("zy", "yz")):
             number = 2 * stage + p
             col_sums[number, getattr(here, order[stage])] = totals_of[p]
-            sums.append(Exchange(here, col_sums.at[number], small_send, small_recv, 7 + number, order[stage]))
+            sums.append(Exchange(here, col_sums.at[number], small_send.at[2], small_recv.at[4 + stage], order[stage]))
             sums[-1].start()
 
     def col_wait(stage):
+        sums[7 + 2 * stage].wait(col_sums.at[2 * stage : 2 * stage + 2, 0:3])
         for p in range(2):
             number = 2 * stage + p
-            sums[7 + number].wait()
             totals_of[p] = merged([col_sums[number, k] for k in range(SIDE)])
 
     col_start(0)
@@ -504,8 +505,9 @@
     col_share.start()
     to_sibling(here, col_out.at[taken], col_out.at[taken], sib_send, sib_recv, 3).wait_recv()
 
-    for exchange in sums:
-        exchange.finish()
+    sums[0].finish(core_sums.at[:, 0:3])
+    rows_x.finish(row_parts.at[0:3])
+    sums[7].finish(col_sums.at[:, 0:3])
     for copy in (core_swap, half_swap, col_swap, col_share):
         copy.wait_send()
 
@@ -594,8 +596,8 @@
             pltpu.SemaphoreType.DMA((Gather.RECEIVES,)),
             pltpu.SemaphoreType.DMA((Gather.SENDS,)),
             pltpu.SemaphoreType.DMA((Gather.RECEIVES,)),
-            pltpu.SemaphoreType.DMA((11,)),
-            pltpu.SemaphoreType.DMA((11,)),
+            pltpu.SemaphoreType.DMA((3,)),
+            pltpu.SemaphoreType.DMA((6,)),
             pltpu.SemaphoreType.DMA((4,)),
             pltpu.SemaphoreType.DMA((4,)),
         ],

time: 60.6 us -> 60.3 us (level)
  no operation moved by 1% of the time
where the time goes in v6:
time: 60.3 us; the launch traced here: 60.2 us
  Pallas kernels  59.5 us (99%)
  between operations  0.64 us (1%)
    pallas_call x1, Pallas kernels, per_device(): pl.pallas_call(main_kernel, name='main', out_shape=[pltpu.VMEM((rows, col...  56.2 us
    pallas_call x1, Pallas kernels, per_device(): pl.pallas_call(functools.partial(plan_kernel, source_count), name='plan',...  3.37 us

profile of v6, /device:TPU:1, one launch (start us, length us, event | category | flops | bytes accessed | tf_op | source)
XLA Modules:
  0.0 60.2 jit_solution(1478452045538079846)
XLA Ops:
  0.6 56.2 %main.1 = (f32[128,15360]{1,0:T(8,128)S(1)}, f32[128,128]{1,0:T(8,128)S(1)}, f32[1,128]{1,0:T(1,128)S(1)}, f32[120,128]{1,0:T(8,128)S(1)}) custom-call(f32[128,15360]{1,0:T(8,128)} %coupling_hbm.1, bf16[4,15360]{1,0:T(4,128)(2,1)} %tgt_right_hbm.1, bf16[4,15360]{1,0:T(4,128)(2,1)} %tgt_left_hbm.1, bf16[128,128]{1,0:T(8,128)(2,1)} %src_left_hbm.1, ...), custom_call_target="tpu_custom_call" | custom-call | tf_op jit(solution)/shard_map/main/pallas_call | solution.py:564
  56.8 3.4 %plan.1 = (f32[128,15360]{1,0:T(8,128)}, f32[1,128]{1,0:T(1,128)}, f32[120,128]{1,0:T(8,128)}) custom-call(f32[128,15360]{1,0:T(8,128)S(1)} %get-tuple-element.10.score, f32[128,128]{1,0:T(8,128)S(1)} %get-tuple-element.11.row_shift, f32[1,128]{1,0:T(1,128)S(1)} %get-tuple-element.12.row_in, f32[120,128]{1,0:T(8,128)S(1)} %get-tuple-element.13.col_in), custom_call_target="tpu_custom_call" | custom-call | tf_op jit(solution)/shard_map/plan/pallas_call | solution.py:610

commit v7 on v5

--- a/solution.py
+++ b/solution.py
@@ -580,7 +580,7 @@
             pltpu.VMEM((2, rank // 2, rank), BF16),
             pltpu.VMEM((rows, LANES), F32),
             pltpu.VMEM((rows, LANES), F32),
-            pltpu.VMEM((SIDE, 8, LANES), F32),
+            pltpu.VMEM((SIDE, 1, LANES), F32),
             pltpu.VMEM((col_rows, LANES), F32),
             pltpu.VMEM((some, LANES), F32),
             pltpu.VMEM((4, SIDE, some // 2, LANES), F32),

time: 60.6 us -> 60.5 us (level)
  no operation moved by 1% of the time
where the time goes in v7:
time: 60.5 us; the launch traced here: 60.4 us
  Pallas kernels  59.7 us (99%)
  between operations  0.64 us (1%)
    pallas_call x1, Pallas kernels, per_device(): pl.pallas_call(main_kernel, name='main', out_shape=[pltpu.VMEM((rows, col...  56.4 us
    pallas_call x1, Pallas kernels, per_device(): pl.pallas_call(functools.partial(plan_kernel, source_count), name='plan',...  3.37 us

profile of v7, /device:TPU:1, one launch (start us, length us, event | category | flops | bytes accessed | tf_op | source)
XLA Modules:
  0.0 60.4 jit_solution(4325615120051888870)
XLA Ops:
  0.6 56.4 %main.1 = (f32[128,15360]{1,0:T(8,128)S(1)}, f32[128,128]{1,0:T(8,128)S(1)}, f32[1,128]{1,0:T(1,128)S(1)}, f32[120,128]{1,0:T(8,128)S(1)}) custom-call(f32[128,15360]{1,0:T(8,128)} %coupling_hbm.1, bf16[4,15360]{1,0:T(4,128)(2,1)} %tgt_right_hbm.1, bf16[4,15360]{1,0:T(4,128)(2,1)} %tgt_left_hbm.1, bf16[128,128]{1,0:T(8,128)(2,1)} %src_left_hbm.1, ...), custom_call_target="tpu_custom_call" | custom-call | tf_op jit(solution)/shard_map/main/pallas_call | solution.py:562
  57.0 3.4 %plan.1 = (f32[128,15360]{1,0:T(8,128)}, f32[1,128]{1,0:T(1,128)}, f32[120,128]{1,0:T(8,128)}) custom-call(f32[128,15360]{1,0:T(8,128)S(1)} %get-tuple-element.10.score, f32[128,128]{1,0:T(8,128)S(1)} %get-tuple-element.11.row_shift, f32[1,128]{1,0:T(1,128)S(1)} %get-tuple-element.12.row_in, f32[120,128]{1,0:T(8,128)S(1)} %get-tuple-element.13.col_in), custom_call_target="tpu_custom_call" | custom-call | tf_op jit(solution)/shard_map/plan/pallas_call | solution.py:608
